TPU v7x, 1024 devices: a whole 4x4x32 slice. The times are simulated.
1024 devices in a mesh: shard: 128 (over z, y), replica: 8 (over x, core).
Axes of the slice: x: 4, y: 4, z: 32, core: 2. Of those that a mesh axis runs over, the one named last changes fastest.
Arguments:
- replica_grads: bfloat16 [8, 4096, 6144], P('replica', 'shard'), may hold values from -5 to 5
- block_row: int32 [96], replicated, may hold values from 0 to 7, as said below
- block_col: int32 [96], replicated, may hold values from 0 to 11, as said below
- block_owner: int32 [96], replicated, may hold values from 0 to 127, as said below
- left_stats: float32 [256, 512, 512], P('shard', 'replica'), as said below
- right_stats: float32 [256, 512, 512], P('shard', 'replica'), as said below
- left_root: bfloat16 [256, 512, 512], P('shard'), as said below
- right_root: bfloat16 [256, 512, 512], P('shard'), as said below
Outputs:
- direction: bfloat16 [256, 512, 512], P('shard', 'replica')
- left_next: float32 [256, 512, 512], P('shard', 'replica')
- right_next: float32 [256, 512, 512], P('shard', 'replica')
Inputs may be any that keep to these rules, and one draw needn't show every extreme that they name: block_row and block_col together name each of the 8 x 12 block positions exactly once. `block_col`: see block_row. `block_owner`: no shard index owns more than 2 blocks, and some index owns exactly 2. `left_stats`: symmetric. `right_stats`: symmetric. `left_root`: symmetric. `right_root`: symmetric.
All inputs are finite; a program needn't handle non-finite values.
Results may differ from a plain program's by a relative error of at most 0.022.
Values may be sent and summed in bfloat16 or wider, within the bound.
No kernel may reach another device: no remote copies, remote signals or barrier semaphores. Data moves between devices by JAX's collectives and lax.ppermute only.
A program may use at most 64 MiB of HBM per device.

v0:
```python
import jax
import jax.numpy as jnp
from jax import lax
from jax.sharding import PartitionSpec as P


def per_device(
    replica_grads, block_row, block_col, block_owner, left_stats, right_stats, left_root, right_root
):
    slots = left_root.shape[0]
    order = left_root.shape[1]
    replicas = lax.axis_size("replica")
    band_rows = order // replicas
    local_rows = replica_grads.shape[1]
    block_cols = replica_grads.shape[2] // order
    replica_id = lax.axis_index("replica")
    partial_sum = (
        replica_grads[0].astype(jnp.float32).reshape(local_rows, block_cols, replicas, band_rows)
    )
    summed = lax.psum(partial_sum.astype(jnp.bfloat16), "replica").astype(jnp.float32)
    banded = lax.dynamic_slice_in_dim(summed, replica_id, 1, 2)
    reduced = banded.reshape(local_rows, block_cols * band_rows).astype(jnp.bfloat16)
    holder = lax.axis_index("shard")
    owned = (block_owner == holder).astype(jnp.int32)
    ranking = jnp.cumsum(owned) - 1
    slot_ids = jnp.arange(slots, dtype=jnp.int32)[:, None]
    chosen = owned[None, :] * (ranking[None, :] == slot_ids).astype(jnp.int32)
    filled = jnp.sum(chosen, axis=1) > 0
    row_index = jnp.sum(chosen * block_row[None, :], axis=1)
    col_index = jnp.sum(chosen * block_col[None, :], axis=1)
    col_select = jnp.arange(block_cols, dtype=jnp.int32)[None, :] == col_index[:, None]
    blank = jnp.zeros((order, band_rows), jnp.bfloat16)
    start_blocks = jnp.zeros((slots, order, band_rows), jnp.bfloat16)
    shard_rows = lax.all_gather(reduced, "shard", axis=0, tiled=True)
    count = shard_rows.shape[0]
    cubes = shard_rows.reshape(count, block_cols, band_rows)

    def place(summed_block, picked, row_block, live):
        columns = jnp.sum(jnp.where(picked[None, :, None], cubes, jnp.zeros_like(cubes)), axis=1)
        padded = jnp.concatenate([blank, columns, blank], axis=0)
        offset = row_block * order
        window = lax.dynamic_slice_in_dim(padded, jnp.clip(offset, -order, count) + order, order, 0)
        row_ids = offset + jnp.arange(order, dtype=jnp.int32)
        usable = (row_ids >= 0) & (row_ids < count) & live
        return summed_block + jnp.where(usable[:, None], window, jnp.zeros_like(window))

    band_cols = jax.vmap(place)(start_blocks, col_select, row_index, filled)
    blocks = lax.all_gather(band_cols, "replica", axis=2, tiled=True)
    my_rows = lax.dynamic_slice_in_dim(blocks, replica_id * band_rows, band_rows, 1)
    gram_left = jnp.einsum("kib,kjb->kij", my_rows, blocks, preferred_element_type=jnp.float32)
    gram_right = jnp.einsum("kai,kaj->kij", band_cols, blocks, preferred_element_type=jnp.float32)
    left_next = 0.8 * left_stats + 0.2 / order * gram_left
    right_next = 0.8 * right_stats + 0.2 / order * gram_right
    mixed = jnp.einsum(
        "kab,kbc->kac", blocks, right_root, preferred_element_type=jnp.float32
    ).astype(jnp.bfloat16)
    root_rows = lax.dynamic_slice_in_dim(left_root, replica_id * band_rows, band_rows, 1)
    direction = jnp.einsum(
        "kab,kbc->kac", root_rows, mixed, preferred_element_type=jnp.float32
    ).astype(jnp.bfloat16)
    return (direction, left_next, right_next)


def solution(mesh):
    in_specs = (
        P("replica", "shard", None),
        P(),
        P(),
        P(),
        P("shard", "replica", None),
        P("shard", "replica", None),
        P("shard", None, None),
        P("shard", None, None),
    )
    out_specs = (
        P("shard", "replica", None),
        P("shard", "replica", None),
        P("shard", "replica", None),
    )
    return jax.shard_map(
        per_device, mesh=mesh, in_specs=in_specs, out_specs=out_specs, check_vma=False
    )
```

profile of v0, /device:TPU:1, one launch (start us, length us, event | category | flops | bytes accessed | tf_op | source)
XLA Modules:
  0.0 502.5 jit_solution(5756781295549947284)
XLA Ops:
  7.2 0.0 copy-start
  7.2 0.0 copy-start.6
  7.2 0.0 copy-start.4
  7.2 0.0 copy-start.5
  7.2 0.0 all-reduce.3.cloned.1.call-start
  7.3 1.8 squeeze.3
  9.1 1.2 copy.25
  10.3 0.0 all-reduce.3.cloned.1.call-update
  10.3 0.0 all-gather.3.cloned.1.call-start
  10.4 106.7 %all-reduce.3.cloned.1.call-done = bf16[32,12,8,64]{3,1,0,2:T(8,128)(2,1)} async-done(((bf16[32,12,8,64]{3,1,0,2:T(8,128)(2,1)}), bf16[32,12,8,64]{3,1,0,2:T(8,128)(2,1)}) %all-reduce.3.cloned.1.call-update) | async-done | bytes 393232 | tf_op jit(solution)/shard_map/psum | solution.py:20
  117.0 0.9 convert_convert_fusion
  118.0 0.7 convert_element_type.27
  118.7 0.0 all-gather.3.cloned.1.call-update
  118.7 0.0 all-gather.5.cloned.1.call-start
  118.8 0.0 copy-done.6
  118.8 0.1 copy.24
  118.9 0.1 reduce-window.8
  119.0 0.1 add_reduce_fusion
  119.2 0.0 copy-done.4
  119.2 0.0 copy-done.5
  119.2 0.2 fusion.6
  119.4 0.1 iota_compare_fusion
  119.4 0.1 and_and_fusion
  119.5 264.2 %all-gather.3.cloned.1.call-done = bf16[4096,768]{1,0:T(8,128)(2,1)} async-done(((bf16[32,768]{1,0:T(8,128)(2,1)}), bf16[4096,768]{1,0:T(8,128)(2,1)}) %all-gather.3.cloned.1.call-update) | async-done | bytes 6291472 | tf_op jit(solution)/shard_map/all_gather | solution.py:34
  383.7 8.8 %copy.26 = bf16[4096,768]{0,1:T(8,128)(2,1)} copy(bf16[4096,768]{1,0:T(8,128)(2,1)} %all-gather.3.cloned.1.call-done) | data formatting | bytes 12582912 | tf_op jit(solution)/shard_map/all_gather | solution.py:34
  392.5 6.6 %select_reduce_fusion = bf16[2,4096,64]{1,2,0:T(8,128)(2,1)} fusion(pred[2,12]{1,0:T(4,128)(4,1)S(1)} %iota_compare_fusion, bf16[4096,12,64]{0,2,1:T(8,128)(2,1)} %bitcast.20), kind=kLoop, calls=%fused_computation.1 | loop fusion | flops 12058624 | bytes 7340056 | tf_op jit(solution)/shard_map/vmap()/reduce_sum | solution.py:39
  399.1 5.0 %copy.28 = bf16[2,4096,64]{2,0,1:T(2,128)(2,1)S(1)} copy(bf16[2,4096,64]{1,2,0:T(8,128)(2,1)} %select_reduce_fusion) | data formatting | bytes 2097152 | tf_op jit(solution)/shard_map/vmap()/reduce_sum | solution.py:39
  404.1 0.1 broadcast.147.clone
  404.2 31.9 %pad_maximum_fusion = bf16[2,5120,64]{2,0,1:T(2,128)(2,1)} fusion(bf16[2,512,64]{2,0,1:T(2,128)(2,1)S(1)} %broadcast.147.clone, bf16[2,4096,64]{2,0,1:T(2,128)(2,1)S(1)} %copy.28), kind=kLoop, calls=%fused_computation.2 | loop fusion | flops 1310720 | bytes 2490368 | tf_op jit(solution)/shard_map/vmap()/concatenate | solution.py:40
  436.2 0.0 copy-start.2
  436.2 0.0 copy-start.3
  436.2 3.0 gather_fusion
  439.1 0.1 copy.30
  439.3 0.7 broadcast_select_fusion
  439.9 0.0 all-gather.5.cloned.1.call-update
  440.0 48.6 %all-gather.5.cloned.1.call-done = bf16[2,512,512]{1,2,0:T(8,128)(2,1)} async-done(((bf16[2,512,64]{1,2,0:T(8,128)(2,1)}), bf16[2,512,512]{1,2,0:T(8,128)(2,1)}) %all-gather.5.cloned.1.call-update) | async-done | bytes 1048592 | tf_op jit(solution)/shard_map/all_gather | solution.py:48
  488.5 0.0 copy-done.2
  488.5 0.0 copy-start.1
  488.5 2.5 fusion.1
  491.1 0.0 copy-done.3
  491.1 2.5 fusion.2
  493.5 0.0 copy-done
  493.5 0.0 copy-done.1
  493.5 2.5 fusion.3
  (5 shorter events, 0.0 us)
Async XLA Ops:
  7.2 486.3 %copy-start = (bf16[2,512,512]{2,1,0:T(8,128)(2,1)S(1)}, bf16[2,512,512]{2,1,0:T(8,128)(2,1)}, u32[]{:S(2)}) copy-start(bf16[2,512,512]{2,1,0:T(8,128)(2,1)} %param.15) | copy-start | bytes 3145732
  7.2 111.6 %copy-start.6 = (s32[96]{0:T(128)S(1)}, s32[96]{0:T(128)}, u32[]{:S(2)}) copy-start(s32[96]{0:T(128)} %param.11) | copy-start | bytes 1156
  7.2 112.0 %copy-start.4 = (s32[96]{0:T(128)S(1)}, s32[96]{0:T(128)}, u32[]{:S(2)}) copy-start(s32[96]{0:T(128)} %param.10) | copy-start | bytes 1156
  7.2 112.0 %copy-start.5 = (s32[96]{0:T(128)S(1)}, s32[96]{0:T(128)}, u32[]{:S(2)}) copy-start(s32[96]{0:T(128)} %param.9) | copy-start | bytes 1156
  7.2 109.8 %all-reduce.3.cloned.1.call-start = ((), (), s32[]{:S(2)}) async-start(), calls=%async_computation | async-start | bytes 2097152 | tf_op jit(solution)/shard_map/psum | solution.py:20
  10.3 373.4 %all-gather.3.cloned.1.call-start = ((), (), s32[]{:S(2)}) async-start(), calls=%async_computation.1 | async-start | bytes 6340608 | tf_op jit(solution)/shard_map/all_gather | solution.py:34
  118.7 369.8 %all-gather.5.cloned.1.call-start = ((), (), s32[]{:S(2)}) async-start(), calls=%async_computation.2 | async-start | bytes 1179648 | tf_op jit(solution)/shard_map/all_gather | solution.py:48
  436.2 52.4 %copy-start.2 = (f32[2,64,512]{2,1,0:T(8,128)S(1)}, f32[2,64,512]{2,1,0:T(8,128)}, u32[]{:S(2)}) copy-start(f32[2,64,512]{2,1,0:T(8,128)} %param.13) | copy-start | bytes 786436
  436.2 54.9 %copy-start.3 = (f32[2,64,512]{2,1,0:T(8,128)S(1)}, f32[2,64,512]{2,1,0:T(8,128)}, u32[]{:S(2)}) copy-start(f32[2,64,512]{2,1,0:T(8,128)} %param.12) | copy-start | bytes 786436
  488.5 5.0 copy-start.1
Sparse Core Ops, SparseCore 0:
  10.5 106.5 all-reduce.2
  121.7 261.9 all-gather.2
  440.1 48.3 all-gather.4
where the time goes:
time: 503 us
  waiting for transfers between devices  419 us (83%)
  other arithmetic  40.6 us (8%)
  local copies, waits for them, and re-layouts  21 us (4%)
  between operations  13.9 us (3%)
  matrix products  7.44 us (1%)
    all_gather x1, waiting for transfers between devices, per_device(): shard_rows = lax.all_gather(reduced, 'shard', axis=0, tiled=True)  264 us
    psum x1, waiting for transfers between devices, per_device(): lax.psum(partial_sum.astype(jnp.bfloat16), 'replica').astype(jnp.float32)  107 us
    all_gather x1, waiting for transfers between devices, per_device(): blocks = lax.all_gather(band_cols, 'replica', axis=2, tiled=True)  48.6 us
    concatenate x1, other arithmetic, place(): padded = jnp.concatenate([blank, columns, blank], axis=0)  31.9 us
  transfers between devices with their start and end apart: 3, of which 3 were waited for; matrix products, arithmetic and copies ran while one was open for 0% of the time, Pallas kernels for 0%

commit v1 on v0

v1 whole, which is shorter than its diff:
```python
import jax
import jax.numpy as jnp
from jax import lax
from jax.experimental import pallas as pl
from jax.experimental.pallas import tpu as pltpu
from jax.sharding import Mesh, PartitionSpec as P

NEAR = ("zl", "y")
TILE_ROWS = 16
LANES = 128


def vmem(n):
    return [pl.BlockSpec(memory_space=pltpu.VMEM)] * n


def cut_kernel(owner_ref, row_ref, col_ref, grads_ref, parts_ref, slot_ref, count_ref, *, near, slots, ncb):
    order = grads_ref.shape[2] // ncb
    groups = order // LANES
    halves = grads_ref.shape[1] // TILE_ROWS
    for group in range(groups):
        for half in range(halves):
            for b in range(ncb):
                parts_ref[group * halves + half, b] = grads_ref[
                    0, pl.ds(half * TILE_ROWS, TILE_ROWS), pl.ds(b * order + group * LANES, LANES)
                ]
    blocks = owner_ref.shape[0]
    base = lax.axis_index("cube") * near

    def clear(i, carry):
        slot_ref[i] = -1
        return carry

    lax.fori_loop(0, slot_ref.shape[0], clear, 0)

    def reset(i, carry):
        count_ref[i] = 0
        return carry

    lax.fori_loop(0, count_ref.shape[0], reset, 0)

    def put(b, carry):
        local = owner_ref[b] - base
        mine = (local >= 0) & (local < near)

        @pl.when(mine)
        def _():
            rank = count_ref[local]
            slot_ref[local * slots + rank] = row_ref[b] * ncb + col_ref[b]
            count_ref[local] = rank + 1

        return carry

    lax.fori_loop(0, blocks, put, 0)


def pick_kernel(slot_ref, shares_ref, picked_ref):
    for s in range(picked_ref.shape[0]):
        at = slot_ref[s]
        tile = shares_ref[jnp.maximum(at, 0)]
        picked_ref[s] = jnp.where(at >= 0, tile, jnp.zeros_like(tile))


def owner_kernel(
    own_ref, other_ref, left_stats_ref, right_stats_ref, left_root_ref, right_root_ref,
    direction_ref, left_ref, right_ref, blocks_ref, columns_ref,
):
    groups, near, slots = own_ref.shape[:3]
    order = blocks_ref.shape[1]
    band = left_ref.shape[1]
    core = lax.axis_index("core")
    me = lax.axis_index("x") * 2 + core
    my_rows = pl.ds(pl.multiple_of(me * band, band), band)
    for k in range(slots):
        for j in range(near):
            for c in range(groups):
                lanes = pl.ds(c * LANES, LANES)
                for half, ref in ((core, own_ref), (1 - core, other_ref)):
                    start = pl.multiple_of(j * 2 * TILE_ROWS + half * TILE_ROWS, TILE_ROWS)
                    blocks_ref[k, pl.ds(start, TILE_ROWS), lanes] = ref[c, j, k]
        block = blocks_ref[k]
        mine = blocks_ref[k, my_rows, :]
        left = lax.dot_general(mine, block, (((1,), (1,)), ((), ())), preferred_element_type=jnp.float32)
        left_ref[k] = 0.8 * left_stats_ref[k] + (0.2 / order) * left
        start = pl.multiple_of((me * band // LANES) * LANES, LANES)
        two_bands = blocks_ref[k, :, pl.ds(start, LANES)]
        columns_ref[...] = lax.dot_general(
            two_bands, block, (((0,), (0,)), ((), ())), preferred_element_type=jnp.float32
        )
        right = columns_ref[pl.ds(pl.multiple_of(me * band - start, band), band), :]
        right_ref[k] = 0.8 * right_stats_ref[k] + (0.2 / order) * right
        mixed = jnp.dot(block, right_root_ref[k], preferred_element_type=jnp.float32).astype(jnp.bfloat16)
        direction_ref[k] = jnp.dot(
            left_root_ref[k, my_rows, :], mixed, preferred_element_type=jnp.float32
        ).astype(jnp.bfloat16)


def per_device(
    replica_grads, block_row, block_col, block_owner, left_stats, right_stats, left_root, right_root
):
    slots, order, _ = left_root.shape
    band = left_stats.shape[1]
    local_rows, cols = replica_grads.shape[1:]
    ncb = cols // order
    groups = lax.axis_size("x")
    replicas = groups * lax.axis_size("core")
    near = lax.axis_size("zl") * lax.axis_size("y")
    cubes = lax.axis_size("cube")
    bf16 = jnp.bfloat16
    smem = pl.BlockSpec(memory_space=pltpu.SMEM)

    parts, slot = pl.pallas_call(
        lambda *refs: cut_kernel(*refs, near=near, slots=slots, ncb=ncb),
        out_shape=(
            jax.ShapeDtypeStruct((replicas, ncb, TILE_ROWS, LANES), bf16),
            jax.ShapeDtypeStruct((near * slots,), jnp.int32),
        ),
        in_specs=[smem] * 3 + vmem(1),
        out_specs=(vmem(1)[0], smem),
        scratch_shapes=[pltpu.SMEM((near,), jnp.int32)],
        name="cut",
    )(block_owner, block_row, block_col, replica_grads)

    received = lax.all_to_all(parts, ("x", "core"), 0, 0, tiled=True)
    summed = jnp.sum(received.astype(jnp.float32), axis=0).astype(bf16)
    shares = lax.all_gather(summed, "cube", axis=0, tiled=True)

    picked = pl.pallas_call(
        pick_kernel,
        out_shape=jax.ShapeDtypeStruct((near * slots, TILE_ROWS, LANES), bf16),
        in_specs=[smem] + vmem(1),
        out_specs=vmem(1)[0],
        name="pick",
    )(slot, shares)

    picked = picked.reshape(near, slots, TILE_ROWS, LANES)
    held = lax.all_to_all(picked, NEAR, 0, 0, tiled=True)
    own = lax.all_gather(held, "x", axis=0, tiled=False)
    other = lax.ppermute(own, "core", [(0, 1), (1, 0)])

    return pl.pallas_call(
        owner_kernel,
        out_shape=(
            jax.ShapeDtypeStruct((slots, band, order), bf16),
            jax.ShapeDtypeStruct((slots, band, order), jnp.float32),
            jax.ShapeDtypeStruct((slots, band, order), jnp.float32),
        ),
        in_specs=vmem(6),
        out_specs=tuple(vmem(3)),
        scratch_shapes=[
            pltpu.VMEM((slots, order, order), bf16),
            pltpu.VMEM((LANES, order), jnp.float32),
        ],
        compiler_params=pltpu.CompilerParams(vmem_limit_bytes=32 * 1024 * 1024),
        name="owner",
    )(own, other, left_stats, right_stats, left_root, right_root)


def solution(mesh):
    fine = Mesh(mesh.devices.reshape(8, 4, 4, 4, 2), ("cube", "zl", "y", "x", "core"))
    shard, replica = ("cube", "zl", "y"), ("x", "core")
    in_specs = (
        P(replica, shard, None),
        P(),
        P(),
        P(),
        P(shard, replica, None),
        P(shard, replica, None),
        P(shard, None, None),
        P(shard, None, None),
    )
    out_specs = (P(shard, replica, None),) * 3
    return jax.shard_map(
        per_device, mesh=fine, in_specs=in_specs, out_specs=out_specs, check_vma=False
    )
```

time: 503 us -> 112 us (0.22)
  waiting for transfers between devices: 419 us -> 1.51 us
  blocking collectives: 0 us -> 88.9 us
  other arithmetic: 40.6 us -> 0.06 us
  local copies, waits for them, and re-layouts: 21 us -> 0.02 us
  between operations: 13.9 us -> 0.68 us
  starting transfers between devices: 0.12 us -> 12.3 us
  Pallas kernels: 0 us -> 7.76 us
  matrix products: 7.44 us -> 0 us
    all_gather x2 -> x0, waiting for transfers between devices: 313 us -> none  [the longest x1 264 us: per_device(): shard_rows = lax.all_gather(reduced, 'shard', axis=0, tiled=True)]
    psum x1 -> x0, waiting for transfers between devices: 107 us -> none  [per_device(): lax.psum(partial_sum.astype(jnp.bfloat16), 'replica').astype(jnp.float32)]
    all_gather x0 -> x2, blocking collectives: none -> 50.6 us  [the longest x1 40.5 us: per_device(): shares = lax.all_gather(summed, 'cube', axis=0, tiled=True)]
    all_to_all x0 -> x2, blocking collectives: none -> 38.2 us  [the longest x1 25.7 us: per_device(): received = lax.all_to_all(parts, ('x', 'core'), 0, 0, tiled=True)]
    concatenate x1 -> x0, other arithmetic: 31.9 us -> none  [place(): padded = jnp.concatenate([blank, columns, blank], axis=0)]
    ppermute x0 -> x1, starting transfers between devices: none -> 12.3 us  [per_device(): other = lax.ppermute(own, 'core', [(0, 1), (1, 0)])]
    all_gather x1 -> x0, local copies, waits for them, and re-layouts: 8.75 us -> none  [per_device(): shard_rows = lax.all_gather(reduced, 'shard', axis=0, tiled=True)]
    pallas_call x0 -> x3, Pallas kernels: none -> 7.76 us  [the longest x1 3.66 us: per_device(): pl.pallas_call(lambda *refs: cut_kernel(*refs, near=near, slots=slots, nc...]
  transfers between devices with their start and end apart: 3 -> 1, of which waited for: 3 -> 1; matrix products, arithmetic and copies ran while one was open for 0% -> 0% of each run, Pallas kernels for 0% -> 0%
where the time goes in v1:
time: 112 us; the launch traced here: 111 us
  blocking collectives  88.9 us (79%)
  starting transfers between devices  12.3 us (11%)
  Pallas kernels  7.76 us (7%)
  waiting for transfers between devices  1.51 us (1%)
    all_gather x1, blocking collectives, per_device(): shares = lax.all_gather(summed, 'cube', axis=0, tiled=True)  40.5 us
    all_to_all x1, blocking collectives, per_device(): received = lax.all_to_all(parts, ('x', 'core'), 0, 0, tiled=True)  25.7 us
    all_to_all x1, blocking collectives, per_device(): held = lax.all_to_all(picked, NEAR, 0, 0, tiled=True)  12.5 us
    ppermute x1, starting transfers between devices, per_device(): other = lax.ppermute(own, 'core', [(0, 1), (1, 0)])  12.3 us
    all_gather x1, blocking collectives, per_device(): own = lax.all_gather(held, 'x', axis=0, tiled=False)  10.2 us
    pallas_call x1, Pallas kernels, per_device(): pl.pallas_call(lambda *refs: cut_kernel(*refs, near=near, slots=slots, nc...  3.66 us
    pallas_call x1, Pallas kernels, per_device(): pl.pallas_call(owner_kernel, out_shape=(jax.ShapeDtypeStruct((slots, band...  2.36 us
  transfers between devices with their start and end apart: 1, of which 1 were waited for; matrix products, arithmetic and copies ran while one was open for 0% of the time, Pallas kernels for 0%

profile of v1, /device:TPU:1, one launch (start us, length us, event | category | flops | bytes accessed | tf_op | source)
XLA Modules:
  0.0 111.2 jit_solution(14053986646513648468)
XLA Ops:
  0.6 3.7 %cut.1 = (bf16[8,12,16,128]{3,2,1,0:T(8,128)(2,1)}, s32[32]{0:T(128)}) custom-call(s32[96]{0:T(128)} %refs_0_.1, s32[96]{0:T(128)} %refs_1_.1, s32[96]{0:T(128)} %refs_2_.1, bf16[1,32,6144]{2,1,0:T(8,128)(2,1)} %refs_3_.1), custom_call_target="tpu_custom_call" | custom-call | tf_op jit(solution)/shard_map/cut/pallas_call | solution.py:112
  4.3 0.0 copy-start.2
  4.3 0.0 copy-start.3
  4.3 25.7 %all_to_all.10 = bf16[8,12,16,128]{3,2,1,0:T(8,128)(2,1)S(1)} all-to-all(bf16[8,12,16,128]{3,2,1,0:T(8,128)(2,1)} %get-tuple-element.6), channel_id=1, replica_groups=mesh['cube'=8,'zl'=4,'y'=4,'x'=4,'core'=2] {'x','core'}, dimensions={0} | all-to-all | bytes 786432 | tf_op jit(solution)/shard_map/all_to_all | solution.py:124
  30.1 0.0 copy-start.1
  30.1 0.1 reduce_sum.12
  30.1 0.0 copy-start
  30.1 40.5 %all_gather.9.shares_ref = bf16[96,16,128]{2,1,0:T(8,128)(2,1)} all-gather(bf16[12,16,128]{2,1,0:T(8,128)(2,1)S(1)} %reduce_sum.12), channel_id=1, replica_groups=mesh['cube'=8,'zl'=4,'y'=4,'x'=4,'core'=2] {'cube'}, dimensions={0}, use_global_device_ids=true | all-gather | bytes 442368 | tf_op jit(solution)/shard_map/all_gather | solution.py:126
  70.6 1.7 %pick.1 = bf16[32,16,128]{2,1,0:T(8,128)(2,1)} custom-call(s32[32]{0:T(128)} %get-tuple-element.5.slot_ref, bf16[96,16,128]{2,1,0:T(8,128)(2,1)} %all_gather.9.shares_ref), custom_call_target="tpu_custom_call" | custom-call | tf_op jit(solution)/shard_map/pick/pallas_call | solution.py:128
  72.3 12.5 %all_to_all.11 = bf16[16,2,16,128]{3,2,1,0:T(8,128)(2,1)S(1)} all-to-all(bf16[16,2,16,128]{3,2,1,0:T(8,128)(2,1)} %bitcast.4), channel_id=1, replica_groups=mesh['cube'=8,'zl'=4,'y'=4,'x'=4,'core'=2] {'zl','y'}, dimensions={0} | all-to-all | bytes 262144 | tf_op jit(solution)/shard_map/all_to_all | solution.py:137
  84.8 10.2 %all-gather = bf16[64,2,16,128]{3,2,1,0:T(8,128)(2,1)S(1)} all-gather(bf16[16,2,16,128]{3,2,1,0:T(8,128)(2,1)S(1)} %all_to_all.11), channel_id=2, replica_groups=mesh['cube'=8,'zl'=4,'y'=4,'x'=4,'core'=2] {'x'}, dimensions={0}, use_global_device_ids=true | all-gather | bytes 655360 | tf_op jit(solution)/shard_map/all_gather | solution.py:138
  95.0 12.3 %collective-permute-start = (bf16[4,16,2,16,128]{4,3,2,1,0:T(8,128)(2,1)S(1)}, bf16[4,16,2,16,128]{4,3,2,1,0:T(8,128)(2,1)S(1)}, u32[]{:S(2)}, u32[]{:S(2)}) collective-permute-start(bf16[4,16,2,16,128]{4,3,2,1,0:T(8,128)(2,1)S(1)} %bitcast.2), channel_id=1, source_target_pairs={{0,1},{1,0},{2,3},{3,2},{4,5},{5,4},{6,7},{7,6},{8,9},{9,8},{10,11... | collective-permute-start | bytes 1572872 | tf_op jit(solution)/shard_map/ppermute | solution.py:139
  107.3 1.5 %collective-permute-done.other_ref = bf16[4,16,2,16,128]{4,3,2,1,0:T(8,128)(2,1)S(1)} collective-permute-done((bf16[4,16,2,16,128]{4,3,2,1,0:T(8,128)(2,1)S(1)}, bf16[4,16,2,16,128]{4,3,2,1,0:T(8,128)(2,1)S(1)}, u32[]{:S(2)}, u32[]{:S(2)}) %collective-permute-start) | collective-permute-done | bytes 524320 | tf_op jit(solution)/shard_map/ppermute | solution.py:139
  108.8 0.0 copy-done.2
  108.8 0.0 copy-done.3
  108.8 0.0 copy-done.1
  108.8 0.0 copy-done
  108.8 2.4 %owner.1 = (bf16[2,64,512]{2,1,0:T(8,128)(2,1)}, f32[2,64,512]{2,1,0:T(8,128)}, f32[2,64,512]{2,1,0:T(8,128)}) custom-call(bf16[4,16,2,16,128]{4,3,2,1,0:T(8,128)(2,1)S(1)} %bitcast.3, bf16[4,16,2,16,128]{4,3,2,1,0:T(8,128)(2,1)S(1)} %collective-permute-done.other_ref, f32[2,64,512]{2,1,0:T(8,128)S(1)} %copy-done.2, f32[2,64,512]{2,1,0:T(8,128)S(1)} %copy-done.3, ...), custom_call_target="tpu_custom_call" | custom-call | tf_op jit(solution)/shard_map/owner/pallas_call | solution.py:141
Async XLA Ops:
  4.3 104.5 %copy-start.2 = (f32[2,64,512]{2,1,0:T(8,128)S(1)}, f32[2,64,512]{2,1,0:T(8,128)}, u32[]{:S(2)}) copy-start(f32[2,64,512]{2,1,0:T(8,128)} %left_stats_ref.1) | copy-start | bytes 786436
  4.3 104.5 %copy-start.3 = (f32[2,64,512]{2,1,0:T(8,128)S(1)}, f32[2,64,512]{2,1,0:T(8,128)}, u32[]{:S(2)}) copy-start(f32[2,64,512]{2,1,0:T(8,128)} %right_stats_ref.1) | copy-start | bytes 786436
  30.1 78.7 %copy-start.1 = (bf16[2,512,512]{2,1,0:T(8,128)(2,1)S(1)}, bf16[2,512,512]{2,1,0:T(8,128)(2,1)}, u32[]{:S(2)}) copy-start(bf16[2,512,512]{2,1,0:T(8,128)(2,1)} %right_root_ref.1) | copy-start | bytes 3145732
  30.1 78.7 %copy-start = (bf16[2,512,512]{2,1,0:T(8,128)(2,1)S(1)}, bf16[2,512,512]{2,1,0:T(8,128)(2,1)}, u32[]{:S(2)}) copy-start(bf16[2,512,512]{2,1,0:T(8,128)(2,1)} %left_root_ref.1) | copy-start | bytes 3145732
  95.0 13.8 %collective-permute-start = (bf16[4,16,2,16,128]{4,3,2,1,0:T(8,128)(2,1)S(1)}, bf16[4,16,2,16,128]{4,3,2,1,0:T(8,128)(2,1)S(1)}, u32[]{:S(2)}, u32[]{:S(2)}) collective-permute-start(bf16[4,16,2,16,128]{4,3,2,1,0:T(8,128)(2,1)S(1)} %bitcast.2), channel_id=1, source_target_pairs={{0,1},{1,0},{2,3},{3,2},{4,5},{5,4},{6,7},{7,6},{8,9},{9,8},{10,11... | collective-permute-start | bytes 1572872 | tf_op jit(solution)/shard_map/ppermute | solution.py:139

commit v2 on v1

--- a/solution.py
+++ b/solution.py
@@ -5,7 +5,6 @@
 from jax.experimental.pallas import tpu as pltpu
 from jax.sharding import Mesh, PartitionSpec as P
 
-NEAR = ("zl", "y")
 TILE_ROWS = 16
 LANES = 128
 
@@ -14,7 +13,39 @@
     return [pl.BlockSpec(memory_space=pltpu.VMEM)] * n
 
 
-def cut_kernel(owner_ref, row_ref, col_ref, grads_ref, parts_ref, slot_ref, count_ref, *, near, slots, ncb):
+def cut_kernel(
+    owner_hbm, row_hbm, col_hbm, grads_hbm, parts_ref, slot_ref,
+    owner_ref, row_ref, col_ref, grads_ref, count_ref, table_sem, grads_sem, *, near, slots, ncb,
+):
+    grads_copy = pltpu.make_async_copy(grads_hbm, grads_ref, grads_sem)
+    grads_copy.start()
+    table_copies = [
+        pltpu.make_async_copy(source, target, table_sem.at[i])
+        for i, (source, target) in enumerate(((owner_hbm, owner_ref), (row_hbm, row_ref), (col_hbm, col_ref)))
+    ]
+    for copy in table_copies:
+        copy.start()
+    for i in range(near * slots):
+        slot_ref[i] = -1
+    for i in range(near):
+        count_ref[i] = 0
+    base = lax.axis_index("cube") * near
+    for copy in table_copies:
+        copy.wait()
+
+    def put(b, carry):
+        local = owner_ref[b] - base
+
+        @pl.when((local >= 0) & (local < near))
+        def _():
+            rank = count_ref[local]
+            slot_ref[local * slots + rank] = row_ref[b] * ncb + col_ref[b]
+            count_ref[local] = rank + 1
+
+        return carry
+
+    lax.fori_loop(0, owner_ref.shape[0], put, 0, unroll=8)
+    grads_copy.wait()
     order = grads_ref.shape[2] // ncb
     groups = order // LANES
     halves = grads_ref.shape[1] // TILE_ROWS
@@ -24,48 +55,24 @@
                 parts_ref[group * halves + half, b] = grads_ref[
                     0, pl.ds(half * TILE_ROWS, TILE_ROWS), pl.ds(b * order + group * LANES, LANES)
                 ]
-    blocks = owner_ref.shape[0]
-    base = lax.axis_index("cube") * near
-
-    def clear(i, carry):
-        slot_ref[i] = -1
-        return carry
-
-    lax.fori_loop(0, slot_ref.shape[0], clear, 0)
-
-    def reset(i, carry):
-        count_ref[i] = 0
-        return carry
-
-    lax.fori_loop(0, count_ref.shape[0], reset, 0)
-
-    def put(b, carry):
-        local = owner_ref[b] - base
-        mine = (local >= 0) & (local < near)
-
-        @pl.when(mine)
-        def _():
-            rank = count_ref[local]
-            slot_ref[local * slots + rank] = row_ref[b] * ncb + col_ref[b]
-            count_ref[local] = rank + 1
-
-        return carry
-
-    lax.fori_loop(0, blocks, put, 0)
 
 
 def pick_kernel(slot_ref, shares_ref, picked_ref):
-    for s in range(picked_ref.shape[0]):
-        at = slot_ref[s]
-        tile = shares_ref[jnp.maximum(at, 0)]
-        picked_ref[s] = jnp.where(at >= 0, tile, jnp.zeros_like(tile))
+    near, groups, slots = picked_ref.shape[:3]
+    for o in range(near):
+        for k in range(slots):
+            at = slot_ref[o * slots + k]
+            tile = shares_ref[jnp.maximum(at, 0)]
+            tile = jnp.where(at >= 0, tile, jnp.zeros_like(tile))
+            for x in range(groups):
+                picked_ref[o, x, k] = tile
 
 
 def owner_kernel(
     own_ref, other_ref, left_stats_ref, right_stats_ref, left_root_ref, right_root_ref,
     direction_ref, left_ref, right_ref, blocks_ref, columns_ref,
 ):
-    groups, near, slots = own_ref.shape[:3]
+    near, groups, slots = own_ref.shape[:3]
     order = blocks_ref.shape[1]
     band = left_ref.shape[1]
     core = lax.axis_index("core")
@@ -77,7 +84,7 @@
                 lanes = pl.ds(c * LANES, LANES)
                 for half, ref in ((core, own_ref), (1 - core, other_ref)):
                     start = pl.multiple_of(j * 2 * TILE_ROWS + half * TILE_ROWS, TILE_ROWS)
-                    blocks_ref[k, pl.ds(start, TILE_ROWS), lanes] = ref[c, j, k]
+                    blocks_ref[k, pl.ds(start, TILE_ROWS), lanes] = ref[j, c, k]
         block = blocks_ref[k]
         mine = blocks_ref[k, my_rows, :]
         left = lax.dot_general(mine, block, (((1,), (1,)), ((), ())), preferred_element_type=jnp.float32)
@@ -115,9 +122,15 @@
             jax.ShapeDtypeStruct((replicas, ncb, TILE_ROWS, LANES), bf16),
             jax.ShapeDtypeStruct((near * slots,), jnp.int32),
         ),
-        in_specs=[smem] * 3 + vmem(1),
+        in_specs=[pl.BlockSpec(memory_space=pl.ANY)] * 4,
         out_specs=(vmem(1)[0], smem),
-        scratch_shapes=[pltpu.SMEM((near,), jnp.int32)],
+        scratch_shapes=[pltpu.SMEM(block_owner.shape, jnp.int32)] * 3
+        + [
+            pltpu.VMEM(replica_grads.shape, bf16),
+            pltpu.SMEM((near,), jnp.int32),
+            pltpu.SemaphoreType.DMA((3,)),
+            pltpu.SemaphoreType.DMA,
+        ],
         name="cut",
     )(block_owner, block_row, block_col, replica_grads)
 
@@ -127,15 +140,15 @@
 
     picked = pl.pallas_call(
         pick_kernel,
-        out_shape=jax.ShapeDtypeStruct((near * slots, TILE_ROWS, LANES), bf16),
+        out_shape=jax.ShapeDtypeStruct((near, groups, slots, TILE_ROWS, LANES), bf16),
         in_specs=[smem] + vmem(1),
         out_specs=vmem(1)[0],
         name="pick",
     )(slot, shares)
 
-    picked = picked.reshape(near, slots, TILE_ROWS, LANES)
-    held = lax.all_to_all(picked, NEAR, 0, 0, tiled=True)
-    own = lax.all_gather(held, "x", axis=0, tiled=False)
+    picked = picked.reshape(near * groups, slots, TILE_ROWS, LANES)
+    own = lax.all_to_all(picked, ("zl", "y", "x"), 0, 0, tiled=True)
+    own = own.reshape(near, groups, slots, TILE_ROWS, LANES)
     other = lax.ppermute(own, "core", [(0, 1), (1, 0)])
 
     return pl.pallas_call(

time: 112 us -> 104 us (0.929)
  blocking collectives: 88.9 us -> 85.2 us
  starting transfers between devices: 12.3 us -> 9.57 us
    all_gather x1 -> x0, blocking collectives: 10.2 us -> none  [per_device(): own = lax.all_gather(held, 'x', axis=0, tiled=False)]
    all_to_all x1, blocking collectives: 12.5 us -> 19.1 us  [per_device(): own = lax.all_to_all(picked, ('zl', 'y', 'x'), 0, 0, tiled=True)]
    ppermute x1, starting transfers between devices: 12.3 us -> 9.57 us  [per_device(): other = lax.ppermute(own, 'core', [(0, 1), (1, 0)])]
    pallas_call x1, Pallas kernels: 3.66 us -> 2.42 us  [per_device(): pl.pallas_call(lambda *refs: cut_kernel(*refs, near=near, slots=slots, nc...]
where the time goes in v2:
time: 104 us
  blocking collectives  85.2 us (82%)
  starting transfers between devices  9.57 us (9%)
  Pallas kernels  6.76 us (6%)
  waiting for transfers between devices  1.51 us (1%)
    all_gather x1, blocking collectives, per_device(): shares = lax.all_gather(summed, 'cube', axis=0, tiled=True)  40.5 us
    all_to_all x1, blocking collectives, per_device(): received = lax.all_to_all(parts, ('x', 'core'), 0, 0, tiled=True)  25.6 us
    all_to_all x1, blocking collectives, per_device(): own = lax.all_to_all(picked, ('zl', 'y', 'x'), 0, 0, tiled=True)  19.1 us
    ppermute x1, starting transfers between devices, per_device(): other = lax.ppermute(own, 'core', [(0, 1), (1, 0)])  9.57 us
    pallas_call x1, Pallas kernels, per_device(): pl.pallas_call(lambda *refs: cut_kernel(*refs, near=near, slots=slots, nc...  2.42 us
    pallas_call x1, Pallas kernels, per_device(): pl.pallas_call(owner_kernel, out_shape=(jax.ShapeDtypeStruct((slots, band...  2.36 us
  transfers between devices with their start and end apart: 1, of which 1 were waited for; matrix products, arithmetic and copies ran while one was open for 0% of the time, Pallas kernels for 0%

profile of v2, /device:TPU:1, one launch (start us, length us, event | category | flops | bytes accessed | tf_op | source)
XLA Modules:
  0.0 103.8 jit_solution(9287524966347941306)
XLA Ops:
  0.6 2.4 %cut.1 = (bf16[8,12,16,128]{3,2,1,0:T(8,128)(2,1)}, s32[32]{0:T(128)}) custom-call(s32[96]{0:T(128)} %refs_0_.1, s32[96]{0:T(128)} %refs_1_.1, s32[96]{0:T(128)} %refs_2_.1, bf16[1,32,6144]{2,1,0:T(8,128)(2,1)} %refs_3_.1), custom_call_target="tpu_custom_call" | custom-call | tf_op jit(solution)/shard_map/cut/pallas_call | solution.py:119
  3.1 25.6 %all_to_all.10 = bf16[8,12,16,128]{3,2,1,0:T(8,128)(2,1)S(1)} all-to-all(bf16[8,12,16,128]{3,2,1,0:T(8,128)(2,1)} %get-tuple-element.6), channel_id=1, replica_groups=mesh['cube'=8,'zl'=4,'y'=4,'x'=4,'core'=2] {'x','core'}, dimensions={0} | all-to-all | bytes 786432 | tf_op jit(solution)/shard_map/all_to_all | solution.py:137
  28.7 0.0 copy-start.3
  28.7 0.1 reduce_sum.12
  28.7 0.0 copy-start.1
  28.7 40.5 %all_gather.3.shares_ref = bf16[96,16,128]{2,1,0:T(8,128)(2,1)} all-gather(bf16[12,16,128]{2,1,0:T(8,128)(2,1)S(1)} %reduce_sum.12), channel_id=1, replica_groups=mesh['cube'=8,'zl'=4,'y'=4,'x'=4,'core'=2] {'cube'}, dimensions={0}, use_global_device_ids=true | all-gather | bytes 442368 | tf_op jit(solution)/shard_map/all_gather | solution.py:139
  69.2 0.0 copy-start
  69.2 2.0 %pick.1 = bf16[16,4,2,16,128]{4,3,2,1,0:T(8,128)(2,1)} custom-call(s32[32]{0:T(128)} %get-tuple-element.5.slot_ref, bf16[96,16,128]{2,1,0:T(8,128)(2,1)} %all_gather.3.shares_ref), custom_call_target="tpu_custom_call" | custom-call | tf_op jit(solution)/shard_map/pick/pallas_call | solution.py:141
  71.2 0.0 copy-start.2
  71.2 19.1 %all_to_all.11 = bf16[64,2,16,128]{3,2,1,0:T(8,128)(2,1)S(1)} all-to-all(bf16[64,2,16,128]{3,2,1,0:T(8,128)(2,1)} %bitcast.4), channel_id=1, replica_groups=mesh['cube'=8,'zl'=4,'y'=4,'x'=4,'core'=2] {'zl','y','x'}, dimensions={0} | all-to-all | bytes 1048576 | tf_op jit(solution)/shard_map/all_to_all | solution.py:150
  90.3 9.6 %collective-permute-start = (bf16[16,4,2,16,128]{4,3,2,1,0:T(8,128)(2,1)S(1)}, bf16[16,4,2,16,128]{4,3,2,1,0:T(8,128)(2,1)S(1)}, u32[]{:S(2)}, u32[]{:S(2)}) collective-permute-start(bf16[16,4,2,16,128]{4,3,2,1,0:T(8,128)(2,1)S(1)} %bitcast.2), channel_id=1, source_target_pairs={{0,1},{1,0},{2,3},{3,2},{4,5},{5,4},{6,7},{7,6},{8,9},{9,8},{10,11... | collective-permute-start | bytes 1572872 | tf_op jit(solution)/shard_map/ppermute | solution.py:152
  99.9 1.5 %collective-permute-done.other_ref = bf16[16,4,2,16,128]{4,3,2,1,0:T(8,128)(2,1)S(1)} collective-permute-done((bf16[16,4,2,16,128]{4,3,2,1,0:T(8,128)(2,1)S(1)}, bf16[16,4,2,16,128]{4,3,2,1,0:T(8,128)(2,1)S(1)}, u32[]{:S(2)}, u32[]{:S(2)}) %collective-permute-start) | collective-permute-done | bytes 524320 | tf_op jit(solution)/shard_map/ppermute | solution.py:152
  101.4 0.0 copy-done.3
  101.4 0.0 copy-done.1
  101.4 0.0 copy-done
  101.4 0.0 copy-done.2
  101.4 2.4 %owner.1 = (bf16[2,64,512]{2,1,0:T(8,128)(2,1)}, f32[2,64,512]{2,1,0:T(8,128)}, f32[2,64,512]{2,1,0:T(8,128)}) custom-call(bf16[16,4,2,16,128]{4,3,2,1,0:T(8,128)(2,1)S(1)} %bitcast.3, bf16[16,4,2,16,128]{4,3,2,1,0:T(8,128)(2,1)S(1)} %collective-permute-done.other_ref, f32[2,64,512]{2,1,0:T(8,128)S(1)} %copy-done.2, f32[2,64,512]{2,1,0:T(8,128)S(1)} %copy-done.3, ...), custom_call_target="tpu_custom_call" | custom-call | tf_op jit(solution)/shard_map/owner/pallas_call | solution.py:154
Async XLA Ops:
  28.7 72.8 %copy-start.3 = (f32[2,64,512]{2,1,0:T(8,128)S(1)}, f32[2,64,512]{2,1,0:T(8,128)}, u32[]{:S(2)}) copy-start(f32[2,64,512]{2,1,0:T(8,128)} %right_stats_ref.1) | copy-start | bytes 786436
  28.7 72.7 %copy-start.1 = (bf16[2,512,512]{2,1,0:T(8,128)(2,1)S(1)}, bf16[2,512,512]{2,1,0:T(8,128)(2,1)}, u32[]{:S(2)}) copy-start(bf16[2,512,512]{2,1,0:T(8,128)(2,1)} %right_root_ref.1) | copy-start | bytes 3145732
  69.2 32.2 %copy-start = (bf16[2,512,512]{2,1,0:T(8,128)(2,1)S(1)}, bf16[2,512,512]{2,1,0:T(8,128)(2,1)}, u32[]{:S(2)}) copy-start(bf16[2,512,512]{2,1,0:T(8,128)(2,1)} %left_root_ref.1) | copy-start | bytes 3145732
  71.2 30.2 %copy-start.2 = (f32[2,64,512]{2,1,0:T(8,128)S(1)}, f32[2,64,512]{2,1,0:T(8,128)}, u32[]{:S(2)}) copy-start(f32[2,64,512]{2,1,0:T(8,128)} %left_stats_ref.1) | copy-start | bytes 786436
  90.3 11.1 %collective-permute-start = (bf16[16,4,2,16,128]{4,3,2,1,0:T(8,128)(2,1)S(1)}, bf16[16,4,2,16,128]{4,3,2,1,0:T(8,128)(2,1)S(1)}, u32[]{:S(2)}, u32[]{:S(2)}) collective-permute-start(bf16[16,4,2,16,128]{4,3,2,1,0:T(8,128)(2,1)S(1)} %bitcast.2), channel_id=1, source_target_pairs={{0,1},{1,0},{2,3},{3,2},{4,5},{5,4},{6,7},{7,6},{8,9},{9,8},{10,11... | collective-permute-start | bytes 1572872 | tf_op jit(solution)/shard_map/ppermute | solution.py:152

commit v3 on v2

--- a/solution.py
+++ b/solution.py
@@ -1,3 +1,5 @@
+import functools
+
 import jax
 import jax.numpy as jnp
 from jax import lax
@@ -25,6 +27,7 @@
     ]
     for copy in table_copies:
         copy.start()
+    halves = grads_ref.shape[1] // TILE_ROWS
     for i in range(near * slots):
         slot_ref[i] = -1
     for i in range(near):
@@ -39,7 +42,7 @@
         @pl.when((local >= 0) & (local < near))
         def _():
             rank = count_ref[local]
-            slot_ref[local * slots + rank] = row_ref[b] * ncb + col_ref[b]
+            slot_ref[local * slots + rank] = row_ref[b] * (halves * ncb) + col_ref[b]
             count_ref[local] = rank + 1
 
         return carry
@@ -48,7 +51,6 @@
     grads_copy.wait()
     order = grads_ref.shape[2] // ncb
     groups = order // LANES
-    halves = grads_ref.shape[1] // TILE_ROWS
     for group in range(groups):
         for half in range(halves):
             for b in range(ncb):
@@ -57,40 +59,41 @@
                 ]
 
 
-def pick_kernel(slot_ref, shares_ref, picked_ref):
-    near, groups, slots = picked_ref.shape[:3]
+def pick_kernel(slot_ref, shares_ref, picked_ref, *, ncb):
+    near, groups, halves = picked_ref.shape[:3]
+    core = lax.axis_index("core")
     for o in range(near):
-        for k in range(slots):
-            at = slot_ref[o * slots + k]
-            tile = shares_ref[jnp.maximum(at, 0)]
+        at = slot_ref[o * 2 + core]
+        for half in range(halves):
+            tile = shares_ref[jnp.maximum(at, 0) + half * ncb]
             tile = jnp.where(at >= 0, tile, jnp.zeros_like(tile))
             for x in range(groups):
-                picked_ref[o, x, k] = tile
+                picked_ref[o, x, half] = tile
 
 
 def owner_kernel(
     own_ref, other_ref, left_stats_ref, right_stats_ref, left_root_ref, right_root_ref,
     direction_ref, left_ref, right_ref, blocks_ref, columns_ref,
 ):
-    near, groups, slots = own_ref.shape[:3]
+    near, groups, halves = own_ref.shape[:3]
     order = blocks_ref.shape[1]
     band = left_ref.shape[1]
     core = lax.axis_index("core")
     me = lax.axis_index("x") * 2 + core
     my_rows = pl.ds(pl.multiple_of(me * band, band), band)
-    for k in range(slots):
+    for k, tiles_ref in ((core, own_ref), (1 - core, other_ref)):
+        block_ref = blocks_ref.at[k]
         for j in range(near):
             for c in range(groups):
-                lanes = pl.ds(c * LANES, LANES)
-                for half, ref in ((core, own_ref), (1 - core, other_ref)):
-                    start = pl.multiple_of(j * 2 * TILE_ROWS + half * TILE_ROWS, TILE_ROWS)
-                    blocks_ref[k, pl.ds(start, TILE_ROWS), lanes] = ref[j, c, k]
-        block = blocks_ref[k]
-        mine = blocks_ref[k, my_rows, :]
+                for half in range(halves):
+                    rows = pl.ds((j * halves + half) * TILE_ROWS, TILE_ROWS)
+                    block_ref[rows, pl.ds(c * LANES, LANES)] = tiles_ref[j, c, half]
+        block = block_ref[...]
+        mine = block_ref[my_rows, :]
         left = lax.dot_general(mine, block, (((1,), (1,)), ((), ())), preferred_element_type=jnp.float32)
         left_ref[k] = 0.8 * left_stats_ref[k] + (0.2 / order) * left
         start = pl.multiple_of((me * band // LANES) * LANES, LANES)
-        two_bands = blocks_ref[k, :, pl.ds(start, LANES)]
+        two_bands = block_ref[:, pl.ds(start, LANES)]
         columns_ref[...] = lax.dot_general(
             two_bands, block, (((0,), (0,)), ((), ())), preferred_element_type=jnp.float32
         )
@@ -109,15 +112,15 @@
     band = left_stats.shape[1]
     local_rows, cols = replica_grads.shape[1:]
     ncb = cols // order
-    groups = lax.axis_size("x")
-    replicas = groups * lax.axis_size("core")
+    groups, halves = lax.axis_size("x"), lax.axis_size("core")
+    replicas = groups * halves
     near = lax.axis_size("zl") * lax.axis_size("y")
     cubes = lax.axis_size("cube")
     bf16 = jnp.bfloat16
     smem = pl.BlockSpec(memory_space=pltpu.SMEM)
 
     parts, slot = pl.pallas_call(
-        lambda *refs: cut_kernel(*refs, near=near, slots=slots, ncb=ncb),
+        functools.partial(cut_kernel, near=near, slots=slots, ncb=ncb),
         out_shape=(
             jax.ShapeDtypeStruct((replicas, ncb, TILE_ROWS, LANES), bf16),
             jax.ShapeDtypeStruct((near * slots,), jnp.int32),
@@ -136,19 +139,19 @@
 
     received = lax.all_to_all(parts, ("x", "core"), 0, 0, tiled=True)
     summed = jnp.sum(received.astype(jnp.float32), axis=0).astype(bf16)
-    shares = lax.all_gather(summed, "cube", axis=0, tiled=True)
+    shares = lax.all_gather(summed, ("cube", "core"), axis=0, tiled=True)
 
     picked = pl.pallas_call(
-        pick_kernel,
-        out_shape=jax.ShapeDtypeStruct((near, groups, slots, TILE_ROWS, LANES), bf16),
+        functools.partial(pick_kernel, ncb=ncb),
+        out_shape=jax.ShapeDtypeStruct((near, groups, halves, TILE_ROWS, LANES), bf16),
         in_specs=[smem] + vmem(1),
         out_specs=vmem(1)[0],
         name="pick",
     )(slot, shares)
 
-    picked = picked.reshape(near * groups, slots, TILE_ROWS, LANES)
+    picked = picked.reshape(near * groups, halves, TILE_ROWS, LANES)
     own = lax.all_to_all(picked, ("zl", "y", "x"), 0, 0, tiled=True)
-    own = own.reshape(near, groups, slots, TILE_ROWS, LANES)
+    own = own.reshape(near, groups, halves, TILE_ROWS, LANES)
     other = lax.ppermute(own, "core", [(0, 1), (1, 0)])
 
     return pl.pallas_call(

time: 104 us -> 101 us (0.971)
  starting transfers between devices: 9.57 us -> 3.74 us
  blocking collectives: 85.2 us -> 87.5 us
    all_to_all x1, blocking collectives: 19.1 us -> 27.4 us  [per_device(): own = lax.all_to_all(picked, ('zl', 'y', 'x'), 0, 0, tiled=True)]
    all_gather x1, blocking collectives: 40.5 us -> 34.5 us  [per_device(): shares = lax.all_gather(summed, ('cube', 'core'), axis=0, tiled=True)]
    ppermute x1, starting transfers between devices: 9.57 us -> 3.74 us  [per_device(): other = lax.ppermute(own, 'core', [(0, 1), (1, 0)])]
where the time goes in v3:
time: 101 us; the launch traced here: 100 us
  blocking collectives  87.5 us (87%)
  Pallas kernels  6.81 us (7%)
  starting transfers between devices  3.74 us (4%)
  waiting for transfers between devices  1.51 us (1%)
    all_gather x1, blocking collectives, per_device(): shares = lax.all_gather(summed, ('cube', 'core'), axis=0, tiled=True)  34.5 us
    all_to_all x1, blocking collectives, per_device(): own = lax.all_to_all(picked, ('zl', 'y', 'x'), 0, 0, tiled=True)  27.4 us
    all_to_all x1, blocking collectives, per_device(): received = lax.all_to_all(parts, ('x', 'core'), 0, 0, tiled=True)  25.6 us
    ppermute x1, starting transfers between devices, per_device(): other = lax.ppermute(own, 'core', [(0, 1), (1, 0)])  3.74 us
    pallas_call x1, Pallas kernels, per_device(): pl.pallas_call(functools.partial(cut_kernel, near=near, slots=slots, ncb=...  2.42 us
    pallas_call x1, Pallas kernels, per_device(): pl.pallas_call(owner_kernel, out_shape=(jax.ShapeDtypeStruct((slots, band...  2.22 us
    pallas_call x1, Pallas kernels, per_device(): pl.pallas_call(functools.partial(pick_kernel, ncb=ncb), out_shape=jax.Sha...  2.18 us
  transfers between devices with their start and end apart: 1, of which 1 were waited for; matrix products, arithmetic and copies ran while one was open for 0% of the time, Pallas kernels for 0%

profile of v3, /device:TPU:1, one launch (start us, length us, event | category | flops | bytes accessed | tf_op | source)
XLA Modules:
  0.0 100.3 jit_solution(5326647368739311049)
XLA Ops:
  0.6 2.4 %cut.1 = (bf16[8,12,16,128]{3,2,1,0:T(8,128)(2,1)}, s32[32]{0:T(128)}) custom-call(s32[96]{0:T(128)} %owner_hbm.1, s32[96]{0:T(128)} %row_hbm.1, s32[96]{0:T(128)} %col_hbm.1, bf16[1,32,6144]{2,1,0:T(8,128)(2,1)} %grads_hbm.1), custom_call_target="tpu_custom_call" | custom-call | tf_op jit(solution)/shard_map/cut/pallas_call | solution.py:122
  3.1 25.6 %all_to_all.10 = bf16[8,12,16,128]{3,2,1,0:T(8,128)(2,1)S(1)} all-to-all(bf16[8,12,16,128]{3,2,1,0:T(8,128)(2,1)} %get-tuple-element.6), channel_id=1, replica_groups=mesh['cube'=8,'zl'=4,'y'=4,'x'=4,'core'=2] {'x','core'}, dimensions={0} | all-to-all | bytes 786432 | tf_op jit(solution)/shard_map/all_to_all | solution.py:140
  28.7 0.1 reduce_sum.12
  28.7 0.0 copy-start.3
  28.7 34.5 %all_gather.3.shares_ref = bf16[192,16,128]{2,1,0:T(8,128)(2,1)} all-gather(bf16[12,16,128]{2,1,0:T(8,128)(2,1)S(1)} %reduce_sum.12), channel_id=1, replica_groups=mesh['cube'=8,'zl'=4,'y'=4,'x'=4,'core'=2] {'cube','core'}, dimensions={0}, use_global_device_ids=true | all-gather | bytes 835584 | tf_op jit(solution)/shard_map/all_gather | solution.py:142
  63.3 0.0 copy-start
  63.3 0.0 copy-start.1
  63.3 2.2 %pick.1 = bf16[16,4,2,16,128]{4,3,2,1,0:T(8,128)(2,1)} custom-call(s32[32]{0:T(128)} %get-tuple-element.5.slot_ref, bf16[192,16,128]{2,1,0:T(8,128)(2,1)} %all_gather.3.shares_ref), custom_call_target="tpu_custom_call" | custom-call | tf_op jit(solution)/shard_map/pick/pallas_call | solution.py:144
  65.4 0.0 copy-start.2
  65.4 27.4 %all_to_all.11 = bf16[64,2,16,128]{3,2,1,0:T(8,128)(2,1)S(1)} all-to-all(bf16[64,2,16,128]{3,2,1,0:T(8,128)(2,1)} %bitcast.4), channel_id=1, replica_groups=mesh['cube'=8,'zl'=4,'y'=4,'x'=4,'core'=2] {'zl','y','x'}, dimensions={0} | all-to-all | bytes 1048576 | tf_op jit(solution)/shard_map/all_to_all | solution.py:153
  92.8 3.7 %collective-permute-start = (bf16[16,4,2,16,128]{4,3,2,1,0:T(8,128)(2,1)S(1)}, bf16[16,4,2,16,128]{4,3,2,1,0:T(8,128)(2,1)S(1)}, u32[]{:S(2)}, u32[]{:S(2)}) collective-permute-start(bf16[16,4,2,16,128]{4,3,2,1,0:T(8,128)(2,1)S(1)} %bitcast.2), channel_id=1, source_target_pairs={{0,1},{1,0},{2,3},{3,2},{4,5},{5,4},{6,7},{7,6},{8,9},{9,8},{10,11... | collective-permute-start | bytes 1572872 | tf_op jit(solution)/shard_map/ppermute | solution.py:155
  96.6 1.5 %collective-permute-done.other_ref = bf16[16,4,2,16,128]{4,3,2,1,0:T(8,128)(2,1)S(1)} collective-permute-done((bf16[16,4,2,16,128]{4,3,2,1,0:T(8,128)(2,1)S(1)}, bf16[16,4,2,16,128]{4,3,2,1,0:T(8,128)(2,1)S(1)}, u32[]{:S(2)}, u32[]{:S(2)}) %collective-permute-start) | collective-permute-done | bytes 524320 | tf_op jit(solution)/shard_map/ppermute | solution.py:155
  98.1 0.0 copy-done.3
  98.1 0.0 copy-done
  98.1 0.0 copy-done.1
  98.1 0.0 copy-done.2
  98.1 2.2 %owner.1 = (bf16[2,64,512]{2,1,0:T(8,128)(2,1)}, f32[2,64,512]{2,1,0:T(8,128)}, f32[2,64,512]{2,1,0:T(8,128)}) custom-call(bf16[16,4,2,16,128]{4,3,2,1,0:T(8,128)(2,1)S(1)} %bitcast.3, bf16[16,4,2,16,128]{4,3,2,1,0:T(8,128)(2,1)S(1)} %collective-permute-done.other_ref, f32[2,64,512]{2,1,0:T(8,128)S(1)} %copy-done.2, f32[2,64,512]{2,1,0:T(8,128)S(1)} %copy-done.3, ...), custom_call_target="tpu_custom_call" | custom-call | tf_op jit(solution)/shard_map/owner/pallas_call | solution.py:157
Async XLA Ops:
  28.7 69.4 %copy-start.3 = (f32[2,64,512]{2,1,0:T(8,128)S(1)}, f32[2,64,512]{2,1,0:T(8,128)}, u32[]{:S(2)}) copy-start(f32[2,64,512]{2,1,0:T(8,128)} %right_stats_ref.1) | copy-start | bytes 786436
  63.3 34.8 %copy-start = (bf16[2,512,512]{2,1,0:T(8,128)(2,1)S(1)}, bf16[2,512,512]{2,1,0:T(8,128)(2,1)}, u32[]{:S(2)}) copy-start(bf16[2,512,512]{2,1,0:T(8,128)(2,1)} %left_root_ref.1) | copy-start | bytes 3145732
  63.3 34.8 %copy-start.1 = (bf16[2,512,512]{2,1,0:T(8,128)(2,1)S(1)}, bf16[2,512,512]{2,1,0:T(8,128)(2,1)}, u32[]{:S(2)}) copy-start(bf16[2,512,512]{2,1,0:T(8,128)(2,1)} %right_root_ref.1) | copy-start | bytes 3145732
  65.4 32.7 %copy-start.2 = (f32[2,64,512]{2,1,0:T(8,128)S(1)}, f32[2,64,512]{2,1,0:T(8,128)}, u32[]{:S(2)}) copy-start(f32[2,64,512]{2,1,0:T(8,128)} %left_stats_ref.1) | copy-start | bytes 786436
  92.8 5.3 %collective-permute-start = (bf16[16,4,2,16,128]{4,3,2,1,0:T(8,128)(2,1)S(1)}, bf16[16,4,2,16,128]{4,3,2,1,0:T(8,128)(2,1)S(1)}, u32[]{:S(2)}, u32[]{:S(2)}) collective-permute-start(bf16[16,4,2,16,128]{4,3,2,1,0:T(8,128)(2,1)S(1)} %bitcast.2), channel_id=1, source_target_pairs={{0,1},{1,0},{2,3},{3,2},{4,5},{5,4},{6,7},{7,6},{8,9},{9,8},{10,11... | collective-permute-start | bytes 1572872 | tf_op jit(solution)/shard_map/ppermute | solution.py:155

commit v4 on v3

--- a/solution.py
+++ b/solution.py
@@ -71,38 +71,109 @@
                 picked_ref[o, x, half] = tile
 
 
-def owner_kernel(
-    own_ref, other_ref, left_stats_ref, right_stats_ref, left_root_ref, right_root_ref,
-    direction_ref, left_ref, right_ref, blocks_ref, columns_ref,
-):
-    near, groups, halves = own_ref.shape[:3]
-    order = blocks_ref.shape[1]
-    band = left_ref.shape[1]
+def owner_kernel(*refs, mine):
+    if mine:
+        tiles_ref, *sources, direction_hbm, left_hbm, right_hbm, stats_ref, roots_ref, right_root_ref = refs[:11]
+        own_stats, own_roots, own_right_root, copy_sem = refs[11:15]
+    else:
+        tiles_ref, own_stats, own_roots, own_right_root, _, _, _, direction_hbm, left_hbm, right_hbm = refs[:10]
+    block_ref, columns_ref, direction_ref, left_ref, right_ref, out_sem = refs[-6:]
+    near, groups, halves = tiles_ref.shape[:3]
+    order = block_ref.shape[0]
+    band = left_ref.shape[0]
     core = lax.axis_index("core")
     me = lax.axis_index("x") * 2 + core
+    k = core if mine else 1 - core
     my_rows = pl.ds(pl.multiple_of(me * band, band), band)
-    for k, tiles_ref in ((core, own_ref), (1 - core, other_ref)):
-        block_ref = blocks_ref.at[k]
-        for j in range(near):
-            for c in range(groups):
-                for half in range(halves):
-                    rows = pl.ds((j * halves + half) * TILE_ROWS, TILE_ROWS)
-                    block_ref[rows, pl.ds(c * LANES, LANES)] = tiles_ref[j, c, half]
-        block = block_ref[...]
-        mine = block_ref[my_rows, :]
-        left = lax.dot_general(mine, block, (((1,), (1,)), ((), ())), preferred_element_type=jnp.float32)
-        left_ref[k] = 0.8 * left_stats_ref[k] + (0.2 / order) * left
-        start = pl.multiple_of((me * band // LANES) * LANES, LANES)
-        two_bands = block_ref[:, pl.ds(start, LANES)]
-        columns_ref[...] = lax.dot_general(
-            two_bands, block, (((0,), (0,)), ((), ())), preferred_element_type=jnp.float32
+    copies = []
+    if mine:
+        left_stats, right_stats, left_root, right_root = sources
+        moves = [
+            (left_stats.at[k], own_stats.at[0]),
+            (right_stats.at[k], own_stats.at[1]),
+            (left_root.at[k, my_rows, :], own_roots),
+            (right_root.at[k], own_right_root),
+            (left_stats.at[1 - k], stats_ref.at[0]),
+            (right_stats.at[1 - k], stats_ref.at[1]),
+            (left_root.at[1 - k, my_rows, :], roots_ref),
+            (right_root.at[1 - k], right_root_ref),
+        ]
+        copies = [pltpu.make_async_copy(src, dst, copy_sem.at[i]) for i, (src, dst) in enumerate(moves)]
+        for copy in copies:
+            copy.start()
+    for j in range(near):
+        for c in range(groups):
+            for half in range(halves):
+                rows = pl.ds((j * halves + half) * TILE_ROWS, TILE_ROWS)
+                block_ref[rows, pl.ds(c * LANES, LANES)] = tiles_ref[j, c, half]
+    block = block_ref[...]
+    results = [
+        pltpu.make_async_copy(src, dst.at[k], out_sem.at[i])
+        for i, (src, dst) in enumerate(
+            ((left_ref, left_hbm), (right_ref, right_hbm), (direction_ref, direction_hbm))
         )
-        right = columns_ref[pl.ds(pl.multiple_of(me * band - start, band), band), :]
-        right_ref[k] = 0.8 * right_stats_ref[k] + (0.2 / order) * right
-        mixed = jnp.dot(block, right_root_ref[k], preferred_element_type=jnp.float32).astype(jnp.bfloat16)
-        direction_ref[k] = jnp.dot(
-            left_root_ref[k, my_rows, :], mixed, preferred_element_type=jnp.float32
-        ).astype(jnp.bfloat16)
+    ]
+    for copy in copies[:4]:
+        copy.wait()
+    rows = block_ref[my_rows, :]
+    left = lax.dot_general(rows, block, (((1,), (1,)), ((), ())), preferred_element_type=jnp.float32)
+    left_ref[...] = 0.8 * own_stats[0] + (0.2 / order) * left
+    results[0].start()
+    start = pl.multiple_of((me * band // LANES) * LANES, LANES)
+    two_bands = block_ref[:, pl.ds(start, LANES)]
+    columns_ref[...] = lax.dot_general(
+        two_bands, block, (((0,), (0,)), ((), ())), preferred_element_type=jnp.float32
+    )
+    right = columns_ref[pl.ds(pl.multiple_of(me * band - start, band), band), :]
+    right_ref[...] = 0.8 * own_stats[1] + (0.2 / order) * right
+    results[1].start()
+    mixed = jnp.dot(block, own_right_root[...], preferred_element_type=jnp.float32).astype(jnp.bfloat16)
+    direction_ref[...] = jnp.dot(
+        own_roots[...], mixed, preferred_element_type=jnp.float32
+    ).astype(jnp.bfloat16)
+    results[2].start()
+    for copy in copies[4:] + results:
+        copy.wait()
+
+
+def owner_call(mine, operands, slots, band, order):
+    bf16, f32 = jnp.bfloat16, jnp.float32
+    hbm = pl.BlockSpec(memory_space=pl.ANY)
+    shapes = ((2, band, order), f32), ((band, order), bf16), ((order, order), bf16)
+    outs = tuple(jax.ShapeDtypeStruct((slots, band, order), t) for t in (bf16, f32, f32))
+    if mine:
+        in_specs = vmem(1) + [hbm] * 4
+        out_shape = outs + tuple(pltpu.VMEM(*shape) for shape in shapes)
+        out_specs = (hbm,) * 3 + tuple(vmem(3))
+        scratch = [pltpu.VMEM(*shape) for shape in shapes] + [pltpu.SemaphoreType.DMA((8,))]
+        aliases = {}
+    else:
+        in_specs = vmem(4) + [hbm] * 3
+        out_shape = outs
+        out_specs = (hbm,) * 3
+        scratch = []
+        aliases = {4: 0, 5: 1, 6: 2}
+    scratch += [
+        pltpu.VMEM((order, order), bf16),
+        pltpu.VMEM((LANES, order), f32),
+        pltpu.VMEM((band, order), bf16),
+        pltpu.VMEM((band, order), f32),
+        pltpu.VMEM((band, order), f32),
+        pltpu.SemaphoreType.DMA((3,)),
+    ]
+    return pl.pallas_call(
+        functools.partial(owner_kernel, mine=mine),
+        out_shape=out_shape,
+        in_specs=in_specs,
+        out_specs=out_specs,
+        scratch_shapes=scratch,
+        input_output_aliases=aliases,
+        compiler_params=pltpu.CompilerParams(vmem_limit_bytes=32 * 1024 * 1024),
+        cost_estimate=pl.CostEstimate(
+            flops=2 * order * order * (order + 4 * band), bytes_accessed=8 * order * order, transcendentals=0
+        ),
+        name="own" if mine else "other",
+    )(*operands)
 
 
 def per_device(
@@ -122,7 +193,7 @@
     parts, slot = pl.pallas_call(
         functools.partial(cut_kernel, near=near, slots=slots, ncb=ncb),
         out_shape=(
-            jax.ShapeDtypeStruct((replicas, ncb, TILE_ROWS, LANES), bf16),
+            pltpu.VMEM((replicas, ncb, TILE_ROWS, LANES), bf16),
             jax.ShapeDtypeStruct((near * slots,), jnp.int32),
         ),
         in_specs=[pl.BlockSpec(memory_space=pl.ANY)] * 4,
@@ -140,10 +211,11 @@
     received = lax.all_to_all(parts, ("x", "core"), 0, 0, tiled=True)
     summed = jnp.sum(received.astype(jnp.float32), axis=0).astype(bf16)
     shares = lax.all_gather(summed, ("cube", "core"), axis=0, tiled=True)
+    shares = pltpu.with_memory_space_constraint(shares, pltpu.VMEM)
 
     picked = pl.pallas_call(
         functools.partial(pick_kernel, ncb=ncb),
-        out_shape=jax.ShapeDtypeStruct((near, groups, halves, TILE_ROWS, LANES), bf16),
+        out_shape=pltpu.VMEM((near, groups, halves, TILE_ROWS, LANES), bf16),
         in_specs=[smem] + vmem(1),
         out_specs=vmem(1)[0],
         name="pick",
@@ -154,22 +226,9 @@
     own = own.reshape(near, groups, halves, TILE_ROWS, LANES)
     other = lax.ppermute(own, "core", [(0, 1), (1, 0)])
 
-    return pl.pallas_call(
-        owner_kernel,
-        out_shape=(
-            jax.ShapeDtypeStruct((slots, band, order), bf16),
-            jax.ShapeDtypeStruct((slots, band, order), jnp.float32),
-            jax.ShapeDtypeStruct((slots, band, order), jnp.float32),
-        ),
-        in_specs=vmem(6),
-        out_specs=tuple(vmem(3)),
-        scratch_shapes=[
-            pltpu.VMEM((slots, order, order), bf16),
-            pltpu.VMEM((LANES, order), jnp.float32),
-        ],
-        compiler_params=pltpu.CompilerParams(vmem_limit_bytes=32 * 1024 * 1024),
-        name="owner",
-    )(own, other, left_stats, right_stats, left_root, right_root)
+    operands = own, left_stats, right_stats, left_root, right_root
+    *results, stats, roots, right = owner_call(True, operands, slots, band, order)
+    return owner_call(False, (other, stats, roots, right, *results), slots, band, order)
 
 
 def solution(mesh):

time: 101 us -> 98.9 us (0.979)
  blocking collectives: 87.5 us -> 86 us
  waiting for transfers between devices: 1.51 us -> 0.01 us
    ppermute x1, waiting for transfers between devices: 1.51 us -> 0.01 us  [per_device(): other = lax.ppermute(own, 'core', [(0, 1), (1, 0)])]
    pallas_call x2 -> x3, Pallas kernels: 4.4 us -> 4.95 us  [the longest x2 4.07 us: owner_call(): pl.pallas_call(functools.partial(owner_kernel, mine=mine), out_shape=out_...]
  transfers between devices with their start and end apart: 1 -> 1, of which waited for: 1 -> 0; matrix products, arithmetic and copies ran while one was open for 0% -> 0% of each run, Pallas kernels for 0% -> 3%
where the time goes in v4:
time: 98.9 us; the launch traced here: 98.6 us
  blocking collectives  86 us (87%)
  Pallas kernels  7.06 us (7%)
  starting transfers between devices  3.74 us (4%)
    all_gather x1, blocking collectives, per_device(): shares = lax.all_gather(summed, ('cube', 'core'), axis=0, tiled=True)  33.9 us
    all_to_all x1, blocking collectives, per_device(): own = lax.all_to_all(picked, ('zl', 'y', 'x'), 0, 0, tiled=True)  27.5 us
    all_to_all x1, blocking collectives, per_device(): received = lax.all_to_all(parts, ('x', 'core'), 0, 0, tiled=True)  24.6 us
    pallas_call x2, Pallas kernels, owner_call(): pl.pallas_call(functools.partial(owner_kernel, mine=mine), out_shape=out_...  4.07 us
    ppermute x1, starting transfers between devices, per_device(): other = lax.ppermute(own, 'core', [(0, 1), (1, 0)])  3.74 us
    pallas_call x1, Pallas kernels, per_device(): pl.pallas_call(functools.partial(cut_kernel, near=near, slots=slots, ncb=...  2.1 us
  transfers between devices with their start and end apart: 1, of which 0 were waited for; matrix products, arithmetic and copies ran while one was open for 0% of the time, Pallas kernels for 3%

profile of v4, /device:TPU:1, one launch (start us, length us, event | category | flops | bytes accessed | tf_op | source)
XLA Modules:
  0.0 98.6 jit_solution(9571148206418439431)
XLA Ops:
  0.6 2.1 %cut.1 = (bf16[8,12,16,128]{3,2,1,0:T(8,128)(2,1)S(1)}, s32[32]{0:T(128)}) custom-call(s32[96]{0:T(128)} %owner_hbm.1, s32[96]{0:T(128)} %row_hbm.1, s32[96]{0:T(128)} %col_hbm.1, bf16[1,32,6144]{2,1,0:T(8,128)(2,1)} %grads_hbm.1), custom_call_target="tpu_custom_call" | custom-call | tf_op jit(solution)/shard_map/cut/pallas_call | solution.py:193
  2.7 24.6 %all_to_all.10 = bf16[8,12,16,128]{3,2,1,0:T(8,128)(2,1)S(1)} all-to-all(bf16[8,12,16,128]{3,2,1,0:T(8,128)(2,1)S(1)} %get-tuple-element.12), channel_id=1, replica_groups=mesh['cube'=8,'zl'=4,'y'=4,'x'=4,'core'=2] {'x','core'}, dimensions={0} | all-to-all | bytes 786432 | tf_op jit(solution)/shard_map/all_to_all | solution.py:211
  27.4 0.1 reduce_sum.12
  27.4 33.9 %all_gather.3.shares_ref = bf16[192,16,128]{2,1,0:T(8,128)(2,1)S(1)} all-gather(bf16[12,16,128]{2,1,0:T(8,128)(2,1)S(1)} %reduce_sum.12), channel_id=1, replica_groups=mesh['cube'=8,'zl'=4,'y'=4,'x'=4,'core'=2] {'cube','core'}, dimensions={0}, use_global_device_ids=true | all-gather | bytes 835584 | tf_op jit(solution)/shard_map/all_gather | solution.py:213
  61.4 0.0 copy-start
  61.4 0.0 copy-start.1
  61.4 0.9 pick.1
  62.3 0.0 copy-start.2
  62.3 27.5 %all_to_all.11 = bf16[64,2,16,128]{3,2,1,0:T(8,128)(2,1)S(1)} all-to-all(bf16[64,2,16,128]{3,2,1,0:T(8,128)(2,1)S(1)} %bitcast.2), channel_id=1, replica_groups=mesh['cube'=8,'zl'=4,'y'=4,'x'=4,'core'=2] {'zl','y','x'}, dimensions={0} | all-to-all | bytes 1048576 | tf_op jit(solution)/shard_map/all_to_all | solution.py:225
  89.7 3.7 %collective-permute-start = (bf16[16,4,2,16,128]{4,3,2,1,0:T(8,128)(2,1)S(1)}, bf16[16,4,2,16,128]{4,3,2,1,0:T(8,128)(2,1)S(1)}, u32[]{:S(2)}, u32[]{:S(2)}) collective-permute-start(bf16[16,4,2,16,128]{4,3,2,1,0:T(8,128)(2,1)S(1)} %bitcast.3), channel_id=1, source_target_pairs={{0,1},{1,0},{2,3},{3,2},{4,5},{5,4},{6,7},{7,6},{8,9},{9,8},{10,11... | collective-permute-start | bytes 1572872 | tf_op jit(solution)/shard_map/ppermute | solution.py:227
  93.5 0.0 copy-done
  93.5 0.0 copy-done.1
  93.5 0.0 copy-done.2
  93.5 0.0 copy-start.3
  93.5 0.9 copy-done.3
  94.5 2.5 %own.1 = (bf16[2,64,512]{2,1,0:T(8,128)(2,1)}, f32[2,64,512]{2,1,0:T(8,128)}, f32[2,64,512]{2,1,0:T(8,128)}, f32[2,64,512]{2,1,0:T(8,128)S(1)}, bf16[64,512]{1,0...) custom-call(bf16[16,4,2,16,128]{4,3,2,1,0:T(8,128)(2,1)S(1)} %bitcast.4, f32[2,64,512]{2,1,0:T(8,128)S(1)} %copy-done.2, ...), custom_call_target="tpu_custom_call" | custom-call | flops 402653184 | bytes 2097152 | tf_op jit(solution)/shard_map/own/pallas_call | solution.py:164
  97.0 0.0 collective-permute-done.refs_0_
  97.0 1.5 %other.1 = (bf16[2,64,512]{2,1,0:T(8,128)(2,1)}, f32[2,64,512]{2,1,0:T(8,128)}, f32[2,64,512]{2,1,0:T(8,128)}) custom-call(bf16[16,4,2,16,128]{4,3,2,1,0:T(8,128)(2,1)S(1)} %collective-permute-done.refs_0_, f32[2,64,512]{2,1,0:T(8,128)S(1)} %get-tuple-element.13.refs_1_, ...), custom_call_target="tpu_custom_call", output_to_operand_aliasing={{0}: (4, {}), {1}: (5, {}), {2}: (6, {})} | custom-call | flops 402653184 | bytes 2097152 | tf_op jit(solution)/shard_map/other/pallas_call | solution.py:164
Async XLA Ops:
  61.4 32.1 %copy-start = (bf16[2,512,512]{2,1,0:T(8,128)(2,1)S(1)}, bf16[2,512,512]{2,1,0:T(8,128)(2,1)}, u32[]{:S(2)}) copy-start(bf16[2,512,512]{2,1,0:T(8,128)(2,1)} %refs_3_.1) | copy-start | bytes 3145732
  61.4 32.1 %copy-start.1 = (bf16[2,512,512]{2,1,0:T(8,128)(2,1)S(1)}, bf16[2,512,512]{2,1,0:T(8,128)(2,1)}, u32[]{:S(2)}) copy-start(bf16[2,512,512]{2,1,0:T(8,128)(2,1)} %refs_4_.1) | copy-start | bytes 3145732
  62.3 31.2 %copy-start.2 = (f32[2,64,512]{2,1,0:T(8,128)S(1)}, f32[2,64,512]{2,1,0:T(8,128)}, u32[]{:S(2)}) copy-start(f32[2,64,512]{2,1,0:T(8,128)} %refs_1_.1) | copy-start | bytes 786436
  89.7 7.3 %collective-permute-start = (bf16[16,4,2,16,128]{4,3,2,1,0:T(8,128)(2,1)S(1)}, bf16[16,4,2,16,128]{4,3,2,1,0:T(8,128)(2,1)S(1)}, u32[]{:S(2)}, u32[]{:S(2)}) collective-permute-start(bf16[16,4,2,16,128]{4,3,2,1,0:T(8,128)(2,1)S(1)} %bitcast.3), channel_id=1, source_target_pairs={{0,1},{1,0},{2,3},{3,2},{4,5},{5,4},{6,7},{7,6},{8,9},{9,8},{10,11... | collective-permute-start | bytes 1572872 | tf_op jit(solution)/shard_map/ppermute | solution.py:227
  93.5 1.0 copy-start.3

commit v5 on v4

--- a/solution.py
+++ b/solution.py
@@ -71,12 +71,14 @@
                 picked_ref[o, x, half] = tile
 
 
-def owner_kernel(*refs, mine):
+def owner_kernel(
+    tiles_ref, left_stats_ref, right_stats_ref, left_root_ref, right_root_ref, *refs, mine
+):
     if mine:
-        tiles_ref, *sources, direction_hbm, left_hbm, right_hbm, stats_ref, roots_ref, right_root_ref = refs[:11]
-        own_stats, own_roots, own_right_root, copy_sem = refs[11:15]
+        direction_hbm, left_hbm, right_hbm, staged_ref, stats_ref, stats_sem = refs[:6]
     else:
-        tiles_ref, own_stats, own_roots, own_right_root, _, _, _, direction_hbm, left_hbm, right_hbm = refs[:10]
+        direction_hbm, left_hbm, right_hbm = refs[3:6]
+        stats_ref = right_stats_ref
     block_ref, columns_ref, direction_ref, left_ref, right_ref, out_sem = refs[-6:]
     near, groups, halves = tiles_ref.shape[:3]
     order = block_ref.shape[0]
@@ -87,18 +89,10 @@
     my_rows = pl.ds(pl.multiple_of(me * band, band), band)
     copies = []
     if mine:
-        left_stats, right_stats, left_root, right_root = sources
-        moves = [
-            (left_stats.at[k], own_stats.at[0]),
-            (right_stats.at[k], own_stats.at[1]),
-            (left_root.at[k, my_rows, :], own_roots),
-            (right_root.at[k], own_right_root),
-            (left_stats.at[1 - k], stats_ref.at[0]),
-            (right_stats.at[1 - k], stats_ref.at[1]),
-            (left_root.at[1 - k, my_rows, :], roots_ref),
-            (right_root.at[1 - k], right_root_ref),
+        copies = [
+            pltpu.make_async_copy(right_stats_ref.at[k], stats_ref, stats_sem.at[0]),
+            pltpu.make_async_copy(right_stats_ref.at[1 - k], staged_ref, stats_sem.at[1]),
         ]
-        copies = [pltpu.make_async_copy(src, dst, copy_sem.at[i]) for i, (src, dst) in enumerate(moves)]
         for copy in copies:
             copy.start()
     for j in range(near):
@@ -113,11 +107,9 @@
             ((left_ref, left_hbm), (right_ref, right_hbm), (direction_ref, direction_hbm))
         )
     ]
-    for copy in copies[:4]:
-        copy.wait()
     rows = block_ref[my_rows, :]
     left = lax.dot_general(rows, block, (((1,), (1,)), ((), ())), preferred_element_type=jnp.float32)
-    left_ref[...] = 0.8 * own_stats[0] + (0.2 / order) * left
+    left_ref[...] = 0.8 * left_stats_ref[k] + (0.2 / order) * left
     results[0].start()
     start = pl.multiple_of((me * band // LANES) * LANES, LANES)
     two_bands = block_ref[:, pl.ds(start, LANES)]
@@ -125,34 +117,34 @@
         two_bands, block, (((0,), (0,)), ((), ())), preferred_element_type=jnp.float32
     )
     right = columns_ref[pl.ds(pl.multiple_of(me * band - start, band), band), :]
-    right_ref[...] = 0.8 * own_stats[1] + (0.2 / order) * right
+    for copy in copies[:1]:
+        copy.wait()
+    right_ref[...] = 0.8 * stats_ref[...] + (0.2 / order) * right
     results[1].start()
-    mixed = jnp.dot(block, own_right_root[...], preferred_element_type=jnp.float32).astype(jnp.bfloat16)
+    mixed = jnp.dot(block, right_root_ref[k], preferred_element_type=jnp.float32).astype(jnp.bfloat16)
     direction_ref[...] = jnp.dot(
-        own_roots[...], mixed, preferred_element_type=jnp.float32
+        left_root_ref[k, my_rows, :], mixed, preferred_element_type=jnp.float32
     ).astype(jnp.bfloat16)
     results[2].start()
-    for copy in copies[4:] + results:
+    for copy in copies[1:] + results:
         copy.wait()
 
 
 def owner_call(mine, operands, slots, band, order):
     bf16, f32 = jnp.bfloat16, jnp.float32
     hbm = pl.BlockSpec(memory_space=pl.ANY)
-    shapes = ((2, band, order), f32), ((band, order), bf16), ((order, order), bf16)
-    outs = tuple(jax.ShapeDtypeStruct((slots, band, order), t) for t in (bf16, f32, f32))
+    out_shape = tuple(jax.ShapeDtypeStruct((slots, band, order), t) for t in (bf16, f32, f32))
+    out_specs = (hbm,) * 3
+    scratch = []
     if mine:
-        in_specs = vmem(1) + [hbm] * 4
-        out_shape = outs + tuple(pltpu.VMEM(*shape) for shape in shapes)
-        out_specs = (hbm,) * 3 + tuple(vmem(3))
-        scratch = [pltpu.VMEM(*shape) for shape in shapes] + [pltpu.SemaphoreType.DMA((8,))]
+        in_specs = vmem(2) + [hbm] + vmem(2)
+        out_shape += (pltpu.VMEM((band, order), f32),)
+        out_specs += tuple(vmem(1))
+        scratch = [pltpu.VMEM((band, order), f32), pltpu.SemaphoreType.DMA((2,))]
         aliases = {}
     else:
-        in_specs = vmem(4) + [hbm] * 3
-        out_shape = outs
-        out_specs = (hbm,) * 3
-        scratch = []
-        aliases = {4: 0, 5: 1, 6: 2}
+        in_specs = vmem(5) + [hbm] * 3
+        aliases = {5: 0, 6: 1, 7: 2}
     scratch += [
         pltpu.VMEM((order, order), bf16),
         pltpu.VMEM((LANES, order), f32),
@@ -226,9 +218,14 @@
     own = own.reshape(near, groups, halves, TILE_ROWS, LANES)
     other = lax.ppermute(own, "core", [(0, 1), (1, 0)])
 
+    left_stats, left_root, right_root = (
+        pltpu.with_memory_space_constraint(a, pltpu.VMEM) for a in (left_stats, left_root, right_root)
+    )
+    right_stats = pltpu.with_memory_space_constraint(right_stats, pltpu.HBM)
     operands = own, left_stats, right_stats, left_root, right_root
-    *results, stats, roots, right = owner_call(True, operands, slots, band, order)
-    return owner_call(False, (other, stats, roots, right, *results), slots, band, order)
+    *results, staged = owner_call(True, operands, slots, band, order)
+    operands = other, left_stats, staged, left_root, right_root
+    return owner_call(False, (*operands, *results), slots, band, order)
 
 
 def solution(mesh):

time: 98.9 us -> 97.6 us (0.987)
  transfers between devices with their start and end apart: 1 -> 1, of which waited for: 0 -> 0; matrix products, arithmetic and copies ran while one was open for 0% -> 0% of each run, Pallas kernels for 3% -> 2%
where the time goes in v5:
time: 97.6 us; the launch traced here: 97.4 us
  blocking collectives  86 us (88%)
  Pallas kernels  6.82 us (7%)
  starting transfers between devices  3.74 us (4%)
    all_gather x1, blocking collectives, per_device(): shares = lax.all_gather(summed, ('cube', 'core'), axis=0, tiled=True)  33.9 us
    all_to_all x1, blocking collectives, per_device(): own = lax.all_to_all(picked, ('zl', 'y', 'x'), 0, 0, tiled=True)  27.5 us
    all_to_all x1, blocking collectives, per_device(): received = lax.all_to_all(parts, ('x', 'core'), 0, 0, tiled=True)  24.6 us
    pallas_call x2, Pallas kernels, owner_call(): pl.pallas_call(functools.partial(owner_kernel, mine=mine), out_shape=out_...  3.83 us
    ppermute x1, starting transfers between devices, per_device(): other = lax.ppermute(own, 'core', [(0, 1), (1, 0)])  3.74 us
    pallas_call x1, Pallas kernels, per_device(): pl.pallas_call(functools.partial(cut_kernel, near=near, slots=slots, ncb=...  2.1 us
  transfers between devices with their start and end apart: 1, of which 0 were waited for; matrix products, arithmetic and copies ran while one was open for 0% of the time, Pallas kernels for 2%

profile of v5, /device:TPU:1, one launch (start us, length us, event | category | flops | bytes accessed | tf_op | source)
XLA Modules:
  0.0 97.4 jit_solution(5075135493932659936)
XLA Ops:
  0.6 2.1 %cut.1 = (bf16[8,12,16,128]{3,2,1,0:T(8,128)(2,1)S(1)}, s32[32]{0:T(128)}) custom-call(s32[96]{0:T(128)} %owner_hbm.1, s32[96]{0:T(128)} %row_hbm.1, s32[96]{0:T(128)} %col_hbm.1, bf16[1,32,6144]{2,1,0:T(8,128)(2,1)} %grads_hbm.1), custom_call_target="tpu_custom_call" | custom-call | tf_op jit(solution)/shard_map/cut/pallas_call | solution.py:185
  2.7 24.6 %all_to_all.10 = bf16[8,12,16,128]{3,2,1,0:T(8,128)(2,1)S(1)} all-to-all(bf16[8,12,16,128]{3,2,1,0:T(8,128)(2,1)S(1)} %get-tuple-element.10), channel_id=1, replica_groups=mesh['cube'=8,'zl'=4,'y'=4,'x'=4,'core'=2] {'x','core'}, dimensions={0} | all-to-all | bytes 786432 | tf_op jit(solution)/shard_map/all_to_all | solution.py:203
  27.4 0.1 reduce_sum.12
  27.4 33.9 %all_gather.3.shares_ref = bf16[192,16,128]{2,1,0:T(8,128)(2,1)S(1)} all-gather(bf16[12,16,128]{2,1,0:T(8,128)(2,1)S(1)} %reduce_sum.12), channel_id=1, replica_groups=mesh['cube'=8,'zl'=4,'y'=4,'x'=4,'core'=2] {'cube','core'}, dimensions={0}, use_global_device_ids=true | all-gather | bytes 835584 | tf_op jit(solution)/shard_map/all_gather | solution.py:205
  61.4 0.0 copy-start
  61.4 0.0 copy-start.1
  61.4 0.9 pick.1
  62.3 0.0 copy-start.2
  62.3 27.5 %all_to_all.11 = bf16[64,2,16,128]{3,2,1,0:T(8,128)(2,1)S(1)} all-to-all(bf16[64,2,16,128]{3,2,1,0:T(8,128)(2,1)S(1)} %bitcast.2), channel_id=1, replica_groups=mesh['cube'=8,'zl'=4,'y'=4,'x'=4,'core'=2] {'zl','y','x'}, dimensions={0} | all-to-all | bytes 1048576 | tf_op jit(solution)/shard_map/all_to_all | solution.py:217
  89.7 3.7 %collective-permute-start = (bf16[16,4,2,16,128]{4,3,2,1,0:T(8,128)(2,1)S(1)}, bf16[16,4,2,16,128]{4,3,2,1,0:T(8,128)(2,1)S(1)}, u32[]{:S(2)}, u32[]{:S(2)}) collective-permute-start(bf16[16,4,2,16,128]{4,3,2,1,0:T(8,128)(2,1)S(1)} %bitcast.3), channel_id=1, source_target_pairs={{0,1},{1,0},{2,3},{3,2},{4,5},{5,4},{6,7},{7,6},{8,9},{9,8},{10,11... | collective-permute-start | bytes 1572872 | tf_op jit(solution)/shard_map/ppermute | solution.py:219
  93.5 0.0 copy-done
  93.5 0.0 copy-done.1
  93.5 0.0 copy-done.2
  93.5 2.3 %own.1 = (bf16[2,64,512]{2,1,0:T(8,128)(2,1)}, f32[2,64,512]{2,1,0:T(8,128)}, f32[2,64,512]{2,1,0:T(8,128)}, f32[64,512]{1,0:T(8,128)S(1)}) custom-call(bf16[16,4,2,16,128]{4,3,2,1,0:T(8,128)(2,1)S(1)} %bitcast.4, f32[2,64,512]{2,1,0:T(8,128)S(1)} %copy-done.2, f32[2,64,512]{2,1,0:T(8,128)} %right_stats_ref.1, bf16[2,512,512]{2,1,0:T(8,128)(2,1)S(1)} %copy-done, ...), custom_call_target="tpu_custom_call" | custom-call | flops 402653184 | bytes 2097152 | tf_op jit(solution)/shard_map/own/pallas_call | solution.py:156
  95.8 0.0 collective-permute-done.tiles_ref
  95.8 1.5 %other.1 = (bf16[2,64,512]{2,1,0:T(8,128)(2,1)}, f32[2,64,512]{2,1,0:T(8,128)}, f32[2,64,512]{2,1,0:T(8,128)}) custom-call(bf16[16,4,2,16,128]{4,3,2,1,0:T(8,128)(2,1)S(1)} %collective-permute-done.tiles_ref, f32[2,64,512]{2,1,0:T(8,128)S(1)} %copy-done.2, ...), custom_call_target="tpu_custom_call", output_to_operand_aliasing={{0}: (5, {}), {1}: (6, {}), {2}: (7, {})} | custom-call | flops 402653184 | bytes 2097152 | tf_op jit(solution)/shard_map/other/pallas_call | solution.py:156
Async XLA Ops:
  61.4 32.1 %copy-start = (bf16[2,512,512]{2,1,0:T(8,128)(2,1)S(1)}, bf16[2,512,512]{2,1,0:T(8,128)(2,1)}, u32[]{:S(2)}) copy-start(bf16[2,512,512]{2,1,0:T(8,128)(2,1)} %left_root_ref.3) | copy-start | bytes 3145732
  61.4 32.1 %copy-start.1 = (bf16[2,512,512]{2,1,0:T(8,128)(2,1)S(1)}, bf16[2,512,512]{2,1,0:T(8,128)(2,1)}, u32[]{:S(2)}) copy-start(bf16[2,512,512]{2,1,0:T(8,128)(2,1)} %right_root_ref.3) | copy-start | bytes 3145732
  62.3 31.2 %copy-start.2 = (f32[2,64,512]{2,1,0:T(8,128)S(1)}, f32[2,64,512]{2,1,0:T(8,128)}, u32[]{:S(2)}) copy-start(f32[2,64,512]{2,1,0:T(8,128)} %left_stats_ref.3) | copy-start | bytes 786436
  89.7 6.1 %collective-permute-start = (bf16[16,4,2,16,128]{4,3,2,1,0:T(8,128)(2,1)S(1)}, bf16[16,4,2,16,128]{4,3,2,1,0:T(8,128)(2,1)S(1)}, u32[]{:S(2)}, u32[]{:S(2)}) collective-permute-start(bf16[16,4,2,16,128]{4,3,2,1,0:T(8,128)(2,1)S(1)} %bitcast.3), channel_id=1, source_target_pairs={{0,1},{1,0},{2,3},{3,2},{4,5},{5,4},{6,7},{7,6},{8,9},{9,8},{10,11... | collective-permute-start | bytes 1572872 | tf_op jit(solution)/shard_map/ppermute | solution.py:219

commit v6 on v5

--- a/solution.py
+++ b/solution.py
@@ -16,8 +16,8 @@
 
 
 def cut_kernel(
-    owner_hbm, row_hbm, col_hbm, grads_hbm, parts_ref, slot_ref,
-    owner_ref, row_ref, col_ref, grads_ref, count_ref, table_sem, grads_sem, *, near, slots, ncb,
+    owner_hbm, row_hbm, col_hbm, grads_hbm, stats_hbm, parts_ref, slot_ref, stats_ref,
+    owner_ref, row_ref, col_ref, grads_ref, count_ref, table_sem, grads_sem, stats_sem, *, near, slots, ncb,
 ):
     grads_copy = pltpu.make_async_copy(grads_hbm, grads_ref, grads_sem)
     grads_copy.start()
@@ -27,10 +27,12 @@
     ]
     for copy in table_copies:
         copy.start()
+    stats_copy = pltpu.make_async_copy(stats_hbm, stats_ref, stats_sem)
+    stats_copy.start()
     halves = grads_ref.shape[1] // TILE_ROWS
-    for i in range(near * slots):
+    for i in range(slot_ref.shape[0]):
         slot_ref[i] = -1
-    for i in range(near):
+    for i in range(count_ref.shape[0]):
         count_ref[i] = 0
     base = lax.axis_index("cube") * near
     for copy in table_copies:
@@ -38,13 +40,11 @@
 
     def put(b, carry):
         local = owner_ref[b] - base
-
-        @pl.when((local >= 0) & (local < near))
-        def _():
-            rank = count_ref[local]
-            slot_ref[local * slots + rank] = row_ref[b] * (halves * ncb) + col_ref[b]
-            count_ref[local] = rank + 1
-
+        mine = (local >= 0) & (local < near)
+        local = jnp.where(mine, local, near)
+        rank = count_ref[local]
+        slot_ref[local * slots + rank] = row_ref[b] * (halves * ncb) + col_ref[b]
+        count_ref[local] = rank + mine.astype(jnp.int32)
         return carry
 
     lax.fori_loop(0, owner_ref.shape[0], put, 0, unroll=8)
@@ -57,6 +57,7 @@
                 parts_ref[group * halves + half, b] = grads_ref[
                     0, pl.ds(half * TILE_ROWS, TILE_ROWS), pl.ds(b * order + group * LANES, LANES)
                 ]
+    stats_copy.wait()
 
 
 def pick_kernel(slot_ref, shares_ref, picked_ref, *, ncb):
@@ -74,11 +75,7 @@
 def owner_kernel(
     tiles_ref, left_stats_ref, right_stats_ref, left_root_ref, right_root_ref, *refs, mine
 ):
-    if mine:
-        direction_hbm, left_hbm, right_hbm, staged_ref, stats_ref, stats_sem = refs[:6]
-    else:
-        direction_hbm, left_hbm, right_hbm = refs[3:6]
-        stats_ref = right_stats_ref
+    direction_hbm, left_hbm, right_hbm = refs[-9:-6]
     block_ref, columns_ref, direction_ref, left_ref, right_ref, out_sem = refs[-6:]
     near, groups, halves = tiles_ref.shape[:3]
     order = block_ref.shape[0]
@@ -87,14 +84,6 @@
     me = lax.axis_index("x") * 2 + core
     k = core if mine else 1 - core
     my_rows = pl.ds(pl.multiple_of(me * band, band), band)
-    copies = []
-    if mine:
-        copies = [
-            pltpu.make_async_copy(right_stats_ref.at[k], stats_ref, stats_sem.at[0]),
-            pltpu.make_async_copy(right_stats_ref.at[1 - k], staged_ref, stats_sem.at[1]),
-        ]
-        for copy in copies:
-            copy.start()
     for j in range(near):
         for c in range(groups):
             for half in range(halves):
@@ -117,35 +106,22 @@
         two_bands, block, (((0,), (0,)), ((), ())), preferred_element_type=jnp.float32
     )
     right = columns_ref[pl.ds(pl.multiple_of(me * band - start, band), band), :]
-    for copy in copies[:1]:
-        copy.wait()
-    right_ref[...] = 0.8 * stats_ref[...] + (0.2 / order) * right
+    right_ref[...] = 0.8 * right_stats_ref[k] + (0.2 / order) * right
     results[1].start()
     mixed = jnp.dot(block, right_root_ref[k], preferred_element_type=jnp.float32).astype(jnp.bfloat16)
     direction_ref[...] = jnp.dot(
         left_root_ref[k, my_rows, :], mixed, preferred_element_type=jnp.float32
     ).astype(jnp.bfloat16)
     results[2].start()
-    for copy in copies[1:] + results:
+    for copy in results:
         copy.wait()
 
 
 def owner_call(mine, operands, slots, band, order):
     bf16, f32 = jnp.bfloat16, jnp.float32
     hbm = pl.BlockSpec(memory_space=pl.ANY)
-    out_shape = tuple(jax.ShapeDtypeStruct((slots, band, order), t) for t in (bf16, f32, f32))
-    out_specs = (hbm,) * 3
-    scratch = []
-    if mine:
-        in_specs = vmem(2) + [hbm] + vmem(2)
-        out_shape += (pltpu.VMEM((band, order), f32),)
-        out_specs += tuple(vmem(1))
-        scratch = [pltpu.VMEM((band, order), f32), pltpu.SemaphoreType.DMA((2,))]
-        aliases = {}
-    else:
-        in_specs = vmem(5) + [hbm] * 3
-        aliases = {5: 0, 6: 1, 7: 2}
-    scratch += [
+    aliases = {} if mine else {5: 0, 6: 1, 7: 2}
+    scratch = [
         pltpu.VMEM((order, order), bf16),
         pltpu.VMEM((LANES, order), f32),
         pltpu.VMEM((band, order), bf16),
@@ -155,9 +131,9 @@
     ]
     return pl.pallas_call(
         functools.partial(owner_kernel, mine=mine),
-        out_shape=out_shape,
-        in_specs=in_specs,
-        out_specs=out_specs,
+        out_shape=tuple(jax.ShapeDtypeStruct((slots, band, order), t) for t in (bf16, f32, f32)),
+        in_specs=vmem(5) + [hbm] * len(aliases),
+        out_specs=(hbm,) * 3,
         scratch_shapes=scratch,
         input_output_aliases=aliases,
         compiler_params=pltpu.CompilerParams(vmem_limit_bytes=32 * 1024 * 1024),
@@ -173,32 +149,32 @@
 ):
     slots, order, _ = left_root.shape
     band = left_stats.shape[1]
-    local_rows, cols = replica_grads.shape[1:]
-    ncb = cols // order
+    ncb = replica_grads.shape[2] // order
     groups, halves = lax.axis_size("x"), lax.axis_size("core")
     replicas = groups * halves
     near = lax.axis_size("zl") * lax.axis_size("y")
-    cubes = lax.axis_size("cube")
     bf16 = jnp.bfloat16
     smem = pl.BlockSpec(memory_space=pltpu.SMEM)
 
-    parts, slot = pl.pallas_call(
+    parts, slot, right_stats = pl.pallas_call(
         functools.partial(cut_kernel, near=near, slots=slots, ncb=ncb),
         out_shape=(
             pltpu.VMEM((replicas, ncb, TILE_ROWS, LANES), bf16),
-            jax.ShapeDtypeStruct((near * slots,), jnp.int32),
+            jax.ShapeDtypeStruct(((near + 1) * slots,), jnp.int32),
+            pltpu.VMEM(right_stats.shape, jnp.float32),
         ),
-        in_specs=[pl.BlockSpec(memory_space=pl.ANY)] * 4,
-        out_specs=(vmem(1)[0], smem),
+        in_specs=[pl.BlockSpec(memory_space=pl.ANY)] * 5,
+        out_specs=(vmem(1)[0], smem, vmem(1)[0]),
         scratch_shapes=[pltpu.SMEM(block_owner.shape, jnp.int32)] * 3
         + [
             pltpu.VMEM(replica_grads.shape, bf16),
-            pltpu.SMEM((near,), jnp.int32),
+            pltpu.SMEM((near + 1,), jnp.int32),
             pltpu.SemaphoreType.DMA((3,)),
+            pltpu.SemaphoreType.DMA,
             pltpu.SemaphoreType.DMA,
         ],
         name="cut",
-    )(block_owner, block_row, block_col, replica_grads)
+    )(block_owner, block_row, block_col, replica_grads, right_stats)
 
     received = lax.all_to_all(parts, ("x", "core"), 0, 0, tiled=True)
     summed = jnp.sum(received.astype(jnp.float32), axis=0).astype(bf16)
@@ -221,11 +197,9 @@
     left_stats, left_root, right_root = (
         pltpu.with_memory_space_constraint(a, pltpu.VMEM) for a in (left_stats, left_root, right_root)
     )
-    right_stats = pltpu.with_memory_space_constraint(right_stats, pltpu.HBM)
-    operands = own, left_stats, right_stats, left_root, right_root
-    *results, staged = owner_call(True, operands, slots, band, order)
-    operands = other, left_stats, staged, left_root, right_root
-    return owner_call(False, (*operands, *results), slots, band, order)
+    operands = left_stats, right_stats, left_root, right_root
+    results = owner_call(True, (own, *operands), slots, band, order)
+    return owner_call(False, (other, *operands, *results), slots, band, order)
 
 
 def solution(mesh):

time: 97.6 us -> 97.7 us (level)
  no operation moved by 1% of the time
where the time goes in v6:
time: 97.7 us; the launch traced here: 97.4 us
  blocking collectives  86 us (88%)
  Pallas kernels  5.91 us (6%)
  starting transfers between devices  3.74 us (4%)
    all_gather x1, blocking collectives, per_device(): shares = lax.all_gather(summed, ('cube', 'core'), axis=0, tiled=True)  33.9 us
    all_to_all x1, blocking collectives, per_device(): own = lax.all_to_all(picked, ('zl', 'y', 'x'), 0, 0, tiled=True)  27.5 us
    all_to_all x1, blocking collectives, per_device(): received = lax.all_to_all(parts, ('x', 'core'), 0, 0, tiled=True)  24.6 us
    ppermute x1, starting transfers between devices, per_device(): other = lax.ppermute(own, 'core', [(0, 1), (1, 0)])  3.74 us
    pallas_call x2, Pallas kernels, owner_call(): pl.pallas_call(functools.partial(owner_kernel, mine=mine), out_shape=tupl...  3.02 us
    pallas_call x1, Pallas kernels, per_device(): pl.pallas_call(functools.partial(cut_kernel, near=near, slots=slots, ncb=...  2.01 us
  transfers between devices with their start and end apart: 1, of which 0 were waited for; matrix products, arithmetic and copies ran while one was open for 0% of the time, Pallas kernels for 2%

profile of v6, /device:TPU:1, one launch (start us, length us, event | category | flops | bytes accessed | tf_op | source)
XLA Modules:
  0.0 97.4 jit_solution(14647267754922971027)
XLA Ops:
  0.6 2.0 %cut.1 = (bf16[8,12,16,128]{3,2,1,0:T(8,128)(2,1)S(1)}, s32[34]{0:T(128)}, f32[2,64,512]{2,1,0:T(8,128)S(1)}) custom-call(s32[96]{0:T(128)} %owner_hbm.1, s32[96]{0:T(128)} %row_hbm.1, s32[96]{0:T(128)} %col_hbm.1, bf16[1,32,6144]{2,1,0:T(8,128)(2,1)} %grads_hbm.1, f32[2,64,512]{2,1,0:T(8,128)} %stats_hbm.1), custom_call_target="tpu_custom_call" | custom-call | tf_op jit(solution)/shard_map/cut/pallas_call | solution.py:159
  2.6 0.0 copy-start.3
  2.7 24.6 %all_to_all.10 = bf16[8,12,16,128]{3,2,1,0:T(8,128)(2,1)S(1)} all-to-all(bf16[8,12,16,128]{3,2,1,0:T(8,128)(2,1)S(1)} %get-tuple-element.10), channel_id=1, replica_groups=mesh['cube'=8,'zl'=4,'y'=4,'x'=4,'core'=2] {'x','core'}, dimensions={0} | all-to-all | bytes 786432 | tf_op jit(solution)/shard_map/all_to_all | solution.py:179
  27.3 0.0 copy-done.3
  27.3 0.1 reduce_sum.12
  27.3 33.9 %all_gather.3.shares_ref = bf16[192,16,128]{2,1,0:T(8,128)(2,1)S(1)} all-gather(bf16[12,16,128]{2,1,0:T(8,128)(2,1)S(1)} %reduce_sum.12), channel_id=1, replica_groups=mesh['cube'=8,'zl'=4,'y'=4,'x'=4,'core'=2] {'cube','core'}, dimensions={0}, use_global_device_ids=true | all-gather | bytes 835584 | tf_op jit(solution)/shard_map/all_gather | solution.py:181
  61.3 0.0 copy-start
  61.3 0.0 copy-start.1
  61.3 0.9 pick.1
  62.2 0.0 copy-start.2
  62.2 27.5 %all_to_all.11 = bf16[64,2,16,128]{3,2,1,0:T(8,128)(2,1)S(1)} all-to-all(bf16[64,2,16,128]{3,2,1,0:T(8,128)(2,1)S(1)} %bitcast.2), channel_id=1, replica_groups=mesh['cube'=8,'zl'=4,'y'=4,'x'=4,'core'=2] {'zl','y','x'}, dimensions={0} | all-to-all | bytes 1048576 | tf_op jit(solution)/shard_map/all_to_all | solution.py:193
  89.7 3.7 %collective-permute-start = (bf16[16,4,2,16,128]{4,3,2,1,0:T(8,128)(2,1)S(1)}, bf16[16,4,2,16,128]{4,3,2,1,0:T(8,128)(2,1)S(1)}, u32[]{:S(2)}, u32[]{:S(2)}) collective-permute-start(bf16[16,4,2,16,128]{4,3,2,1,0:T(8,128)(2,1)S(1)} %bitcast.3), channel_id=1, source_target_pairs={{0,1},{1,0},{2,3},{3,2},{4,5},{5,4},{6,7},{7,6},{8,9},{9,8},{10,11... | collective-permute-start | bytes 1572872 | tf_op jit(solution)/shard_map/ppermute | solution.py:195
  93.4 0.0 copy-done
  93.4 0.0 copy-done.1
  93.4 0.0 copy-done.2
  93.4 0.0 copy-start.4
  93.5 0.9 copy-done.4
  94.4 1.5 %own.1 = (bf16[2,64,512]{2,1,0:T(8,128)(2,1)}, f32[2,64,512]{2,1,0:T(8,128)}, f32[2,64,512]{2,1,0:T(8,128)}) custom-call(bf16[16,4,2,16,128]{4,3,2,1,0:T(8,128)(2,1)S(1)} %bitcast.4, f32[2,64,512]{2,1,0:T(8,128)S(1)} %copy-done.2, f32[2,64,512]{2,1,0:T(8,128)S(1)} %copy-done.4, bf16[2,512,512]{2,1,0:T(8,128)(2,1)S(1)} %copy-done, ...), custom_call_target="tpu_custom_call" | custom-call | flops 402653184 | bytes 2097152 | tf_op jit(solution)/shard_map/own/pallas_call | solution.py:132
  95.9 0.0 collective-permute-done.tiles_ref
  95.9 1.5 %other.1 = (bf16[2,64,512]{2,1,0:T(8,128)(2,1)}, f32[2,64,512]{2,1,0:T(8,128)}, f32[2,64,512]{2,1,0:T(8,128)}) custom-call(bf16[16,4,2,16,128]{4,3,2,1,0:T(8,128)(2,1)S(1)} %collective-permute-done.tiles_ref, f32[2,64,512]{2,1,0:T(8,128)S(1)} %copy-done.2, f32[2,64,512]{2,1,0:T(8,128)S(1)} %copy-done.4, ...), custom_call_target="tpu_custom_call", output_to_operand_aliasing={{0}: (5, {}), {1}: (6, {}), {2}: (7, {})} | custom-call | flops 402653184 | bytes 2097152 | tf_op jit(solution)/shard_map/other/pallas_call | solution.py:132
Async XLA Ops:
  2.6 24.6 %copy-start.3 = (f32[2,64,512]{2,1,0:T(8,128)}, f32[2,64,512]{2,1,0:T(8,128)S(1)}, u32[]{:S(2)}) copy-start(f32[2,64,512]{2,1,0:T(8,128)S(1)} %get-tuple-element.11.right_stats_ref) | copy-start | bytes 786436
  61.3 32.1 %copy-start = (bf16[2,512,512]{2,1,0:T(8,128)(2,1)S(1)}, bf16[2,512,512]{2,1,0:T(8,128)(2,1)}, u32[]{:S(2)}) copy-start(bf16[2,512,512]{2,1,0:T(8,128)(2,1)} %left_root_ref.3) | copy-start | bytes 3145732
  61.3 32.1 %copy-start.1 = (bf16[2,512,512]{2,1,0:T(8,128)(2,1)S(1)}, bf16[2,512,512]{2,1,0:T(8,128)(2,1)}, u32[]{:S(2)}) copy-start(bf16[2,512,512]{2,1,0:T(8,128)(2,1)} %right_root_ref.3) | copy-start | bytes 3145732
  62.2 31.2 %copy-start.2 = (f32[2,64,512]{2,1,0:T(8,128)S(1)}, f32[2,64,512]{2,1,0:T(8,128)}, u32[]{:S(2)}) copy-start(f32[2,64,512]{2,1,0:T(8,128)} %left_stats_ref.3) | copy-start | bytes 786436
  89.7 6.2 %collective-permute-start = (bf16[16,4,2,16,128]{4,3,2,1,0:T(8,128)(2,1)S(1)}, bf16[16,4,2,16,128]{4,3,2,1,0:T(8,128)(2,1)S(1)}, u32[]{:S(2)}, u32[]{:S(2)}) collective-permute-start(bf16[16,4,2,16,128]{4,3,2,1,0:T(8,128)(2,1)S(1)} %bitcast.3), channel_id=1, source_target_pairs={{0,1},{1,0},{2,3},{3,2},{4,5},{5,4},{6,7},{7,6},{8,9},{9,8},{10,11... | collective-permute-start | bytes 1572872 | tf_op jit(solution)/shard_map/ppermute | solution.py:195
  93.4 1.0 copy-start.4

commit v7 on v6

--- a/solution.py
+++ b/solution.py
@@ -16,8 +16,8 @@
 
 
 def cut_kernel(
-    owner_hbm, row_hbm, col_hbm, grads_hbm, stats_hbm, parts_ref, slot_ref, stats_ref,
-    owner_ref, row_ref, col_ref, grads_ref, count_ref, table_sem, grads_sem, stats_sem, *, near, slots, ncb,
+    owner_hbm, row_hbm, col_hbm, grads_hbm, parts_ref, slot_ref,
+    owner_ref, row_ref, col_ref, grads_ref, count_ref, table_sem, grads_sem, *, near, slots, ncb,
 ):
     grads_copy = pltpu.make_async_copy(grads_hbm, grads_ref, grads_sem)
     grads_copy.start()
@@ -27,8 +27,6 @@
     ]
     for copy in table_copies:
         copy.start()
-    stats_copy = pltpu.make_async_copy(stats_hbm, stats_ref, stats_sem)
-    stats_copy.start()
     halves = grads_ref.shape[1] // TILE_ROWS
     for i in range(slot_ref.shape[0]):
         slot_ref[i] = -1
@@ -57,10 +55,11 @@
                 parts_ref[group * halves + half, b] = grads_ref[
                     0, pl.ds(half * TILE_ROWS, TILE_ROWS), pl.ds(b * order + group * LANES, LANES)
                 ]
-    stats_copy.wait()
-
-
-def pick_kernel(slot_ref, shares_ref, picked_ref, *, ncb):
+
+
+def pick_kernel(slot_ref, shares_ref, stats_hbm, picked_ref, stats_ref, stats_sem, *, ncb):
+    stats_copy = pltpu.make_async_copy(stats_hbm, stats_ref, stats_sem)
+    stats_copy.start()
     near, groups, halves = picked_ref.shape[:3]
     core = lax.axis_index("core")
     for o in range(near):
@@ -70,6 +69,7 @@
             tile = jnp.where(at >= 0, tile, jnp.zeros_like(tile))
             for x in range(groups):
                 picked_ref[o, x, half] = tile
+    stats_copy.wait()
 
 
 def owner_kernel(
@@ -156,48 +156,50 @@
     bf16 = jnp.bfloat16
     smem = pl.BlockSpec(memory_space=pltpu.SMEM)
 
-    parts, slot, right_stats = pl.pallas_call(
+    parts, slot = pl.pallas_call(
         functools.partial(cut_kernel, near=near, slots=slots, ncb=ncb),
         out_shape=(
             pltpu.VMEM((replicas, ncb, TILE_ROWS, LANES), bf16),
             jax.ShapeDtypeStruct(((near + 1) * slots,), jnp.int32),
-            pltpu.VMEM(right_stats.shape, jnp.float32),
         ),
-        in_specs=[pl.BlockSpec(memory_space=pl.ANY)] * 5,
-        out_specs=(vmem(1)[0], smem, vmem(1)[0]),
+        in_specs=[pl.BlockSpec(memory_space=pl.ANY)] * 4,
+        out_specs=(vmem(1)[0], smem),
         scratch_shapes=[pltpu.SMEM(block_owner.shape, jnp.int32)] * 3
         + [
             pltpu.VMEM(replica_grads.shape, bf16),
             pltpu.SMEM((near + 1,), jnp.int32),
             pltpu.SemaphoreType.DMA((3,)),
             pltpu.SemaphoreType.DMA,
-            pltpu.SemaphoreType.DMA,
         ],
         name="cut",
-    )(block_owner, block_row, block_col, replica_grads, right_stats)
+    )(block_owner, block_row, block_col, replica_grads)
 
     received = lax.all_to_all(parts, ("x", "core"), 0, 0, tiled=True)
     summed = jnp.sum(received.astype(jnp.float32), axis=0).astype(bf16)
     shares = lax.all_gather(summed, ("cube", "core"), axis=0, tiled=True)
     shares = pltpu.with_memory_space_constraint(shares, pltpu.VMEM)
 
-    picked = pl.pallas_call(
+    picked, right_stats = pl.pallas_call(
         functools.partial(pick_kernel, ncb=ncb),
-        out_shape=pltpu.VMEM((near, groups, halves, TILE_ROWS, LANES), bf16),
-        in_specs=[smem] + vmem(1),
-        out_specs=vmem(1)[0],
+        out_shape=(
+            pltpu.VMEM((near, groups, halves, TILE_ROWS, LANES), bf16),
+            pltpu.VMEM(right_stats.shape, jnp.float32),
+        ),
+        in_specs=[smem] + vmem(1) + [pl.BlockSpec(memory_space=pl.ANY)],
+        out_specs=tuple(vmem(2)),
+        scratch_shapes=[pltpu.SemaphoreType.DMA],
         name="pick",
-    )(slot, shares)
+    )(slot, shares, right_stats)
 
     picked = picked.reshape(near * groups, halves, TILE_ROWS, LANES)
     own = lax.all_to_all(picked, ("zl", "y", "x"), 0, 0, tiled=True)
     own = own.reshape(near, groups, halves, TILE_ROWS, LANES)
     other = lax.ppermute(own, "core", [(0, 1), (1, 0)])
 
-    left_stats, left_root, right_root = (
-        pltpu.with_memory_space_constraint(a, pltpu.VMEM) for a in (left_stats, left_root, right_root)
-    )
-    operands = left_stats, right_stats, left_root, right_root
+    operands = tuple(
+        pltpu.with_memory_space_constraint(a, pltpu.VMEM)
+        for a in (left_stats, right_stats, left_root, right_root)
+    )
     results = owner_call(True, (own, *operands), slots, band, order)
     return owner_call(False, (other, *operands, *results), slots, band, order)
 

time: 97.7 us -> 97.7 us (level)
  no operation moved by 1% of the time
where the time goes in v7:
time: 97.7 us; the launch traced here: 97.4 us
  blocking collectives  86.2 us (88%)
  Pallas kernels  6.72 us (7%)
  starting transfers between devices  3.74 us (4%)
    all_gather x1, blocking collectives, per_device(): shares = lax.all_gather(summed, ('cube', 'core'), axis=0, tiled=True)  34.1 us
    all_to_all x1, blocking collectives, per_device(): own = lax.all_to_all(picked, ('zl', 'y', 'x'), 0, 0, tiled=True)  27.5 us
    all_to_all x1, blocking collectives, per_device(): received = lax.all_to_all(parts, ('x', 'core'), 0, 0, tiled=True)  24.6 us
    ppermute x1, starting transfers between devices, per_device(): other = lax.ppermute(own, 'core', [(0, 1), (1, 0)])  3.74 us
    pallas_call x2, Pallas kernels, owner_call(): pl.pallas_call(functools.partial(owner_kernel, mine=mine), out_shape=tupl...  3.03 us
  transfers between devices with their start and end apart: 1, of which 0 were waited for; matrix products, arithmetic and copies ran while one was open for 0% of the time, Pallas kernels for 2%

profile of v7, /device:TPU:1, one launch (start us, length us, event | category | flops | bytes accessed | tf_op | source)
XLA Modules:
  0.0 97.4 jit_solution(4310942070603018555)
XLA Ops:
  0.6 1.9 %cut.1 = (bf16[8,12,16,128]{3,2,1,0:T(8,128)(2,1)S(1)}, s32[34]{0:T(128)}) custom-call(s32[96]{0:T(128)} %owner_hbm.1, s32[96]{0:T(128)} %row_hbm.1, s32[96]{0:T(128)} %col_hbm.1, bf16[1,32,6144]{2,1,0:T(8,128)(2,1)} %grads_hbm.1), custom_call_target="tpu_custom_call" | custom-call | tf_op jit(solution)/shard_map/cut/pallas_call | solution.py:159
  2.6 24.6 %all_to_all.10 = bf16[8,12,16,128]{3,2,1,0:T(8,128)(2,1)S(1)} all-to-all(bf16[8,12,16,128]{3,2,1,0:T(8,128)(2,1)S(1)} %get-tuple-element.11), channel_id=1, replica_groups=mesh['cube'=8,'zl'=4,'y'=4,'x'=4,'core'=2] {'x','core'}, dimensions={0} | all-to-all | bytes 786432 | tf_op jit(solution)/shard_map/all_to_all | solution.py:177
  27.2 0.1 reduce_sum.12
  27.3 0.0 copy-start.2
  27.3 34.1 %all_gather.3.shares_ref = bf16[192,16,128]{2,1,0:T(8,128)(2,1)S(1)} all-gather(bf16[12,16,128]{2,1,0:T(8,128)(2,1)S(1)} %reduce_sum.12), channel_id=1, replica_groups=mesh['cube'=8,'zl'=4,'y'=4,'x'=4,'core'=2] {'cube','core'}, dimensions={0}, use_global_device_ids=true | all-gather | bytes 835584 | tf_op jit(solution)/shard_map/all_gather | solution.py:179
  61.3 0.0 copy-start
  61.3 1.8 %pick.1 = (bf16[16,4,2,16,128]{4,3,2,1,0:T(8,128)(2,1)S(1)}, f32[2,64,512]{2,1,0:T(8,128)S(1)}) custom-call(s32[34]{0:T(128)} %get-tuple-element.10.slot_ref, bf16[192,16,128]{2,1,0:T(8,128)(2,1)S(1)} %all_gather.3.shares_ref, f32[2,64,512]{2,1,0:T(8,128)} %stats_hbm.1), custom_call_target="tpu_custom_call" | custom-call | tf_op jit(solution)/shard_map/pick/pallas_call | solution.py:182
  63.1 0.0 copy-start.1
  63.1 27.5 %all_to_all.11 = bf16[64,2,16,128]{3,2,1,0:T(8,128)(2,1)S(1)} all-to-all(bf16[64,2,16,128]{3,2,1,0:T(8,128)(2,1)S(1)} %bitcast.4), channel_id=1, replica_groups=mesh['cube'=8,'zl'=4,'y'=4,'x'=4,'core'=2] {'zl','y','x'}, dimensions={0} | all-to-all | bytes 1048576 | tf_op jit(solution)/shard_map/all_to_all | solution.py:195
  90.6 3.7 %collective-permute-start = (bf16[16,4,2,16,128]{4,3,2,1,0:T(8,128)(2,1)S(1)}, bf16[16,4,2,16,128]{4,3,2,1,0:T(8,128)(2,1)S(1)}, u32[]{:S(2)}, u32[]{:S(2)}) collective-permute-start(bf16[16,4,2,16,128]{4,3,2,1,0:T(8,128)(2,1)S(1)} %bitcast.2), channel_id=1, source_target_pairs={{0,1},{1,0},{2,3},{3,2},{4,5},{5,4},{6,7},{7,6},{8,9},{9,8},{10,11... | collective-permute-start | bytes 1572872 | tf_op jit(solution)/shard_map/ppermute | solution.py:197
  94.3 0.0 copy-done.2
  94.3 0.0 copy-done
  94.3 0.0 copy-done.1
  94.4 1.5 %own.1 = (bf16[2,64,512]{2,1,0:T(8,128)(2,1)}, f32[2,64,512]{2,1,0:T(8,128)}, f32[2,64,512]{2,1,0:T(8,128)}) custom-call(bf16[16,4,2,16,128]{4,3,2,1,0:T(8,128)(2,1)S(1)} %bitcast.3, f32[2,64,512]{2,1,0:T(8,128)S(1)} %copy-done.2, f32[2,64,512]{2,1,0:T(8,128)S(1)} %get-tuple-element.13.right_stats_ref, bf16[2,512,512]{2,1,0:T(8,128)(2,1)S(1)} %copy-done, ...), custom_call_target="tpu_custom_call" | custom-call | flops 402653184 | bytes 2097152 | tf_op jit(solution)/shard_map/own/pallas_call | solution.py:132
  95.9 0.0 collective-permute-done.tiles_ref
  95.9 1.5 %other.1 = (bf16[2,64,512]{2,1,0:T(8,128)(2,1)}, f32[2,64,512]{2,1,0:T(8,128)}, f32[2,64,512]{2,1,0:T(8,128)}) custom-call(bf16[16,4,2,16,128]{4,3,2,1,0:T(8,128)(2,1)S(1)} %collective-permute-done.tiles_ref, f32[2,64,512]{2,1,0:T(8,128)S(1)} %copy-done.2, ...), custom_call_target="tpu_custom_call", output_to_operand_aliasing={{0}: (5, {}), {1}: (6, {}), {2}: (7, {})} | custom-call | flops 402653184 | bytes 2097152 | tf_op jit(solution)/shard_map/other/pallas_call | solution.py:132
Async XLA Ops:
  27.3 67.1 %copy-start.2 = (f32[2,64,512]{2,1,0:T(8,128)S(1)}, f32[2,64,512]{2,1,0:T(8,128)}, u32[]{:S(2)}) copy-start(f32[2,64,512]{2,1,0:T(8,128)} %left_stats_ref.3) | copy-start | bytes 786436
  61.3 33.0 %copy-start = (bf16[2,512,512]{2,1,0:T(8,128)(2,1)S(1)}, bf16[2,512,512]{2,1,0:T(8,128)(2,1)}, u32[]{:S(2)}) copy-start(bf16[2,512,512]{2,1,0:T(8,128)(2,1)} %left_root_ref.3) | copy-start | bytes 3145732
  63.1 31.2 %copy-start.1 = (bf16[2,512,512]{2,1,0:T(8,128)(2,1)S(1)}, bf16[2,512,512]{2,1,0:T(8,128)(2,1)}, u32[]{:S(2)}) copy-start(bf16[2,512,512]{2,1,0:T(8,128)(2,1)} %right_root_ref.3) | copy-start | bytes 3145732
  90.6 5.3 %collective-permute-start = (bf16[16,4,2,16,128]{4,3,2,1,0:T(8,128)(2,1)S(1)}, bf16[16,4,2,16,128]{4,3,2,1,0:T(8,128)(2,1)S(1)}, u32[]{:S(2)}, u32[]{:S(2)}) collective-permute-start(bf16[16,4,2,16,128]{4,3,2,1,0:T(8,128)(2,1)S(1)} %bitcast.2), channel_id=1, source_target_pairs={{0,1},{1,0},{2,3},{3,2},{4,5},{5,4},{6,7},{7,6},{8,9},{9,8},{10,11... | collective-permute-start | bytes 1572872 | tf_op jit(solution)/shard_map/ppermute | solution.py:197

commit v8 on v5

--- a/solution.py
+++ b/solution.py
@@ -28,9 +28,9 @@
     for copy in table_copies:
         copy.start()
     halves = grads_ref.shape[1] // TILE_ROWS
-    for i in range(near * slots):
+    for i in range(slot_ref.shape[0]):
         slot_ref[i] = -1
-    for i in range(near):
+    for i in range(count_ref.shape[0]):
         count_ref[i] = 0
     base = lax.axis_index("cube") * near
     for copy in table_copies:
@@ -38,13 +38,11 @@
 
     def put(b, carry):
         local = owner_ref[b] - base
-
-        @pl.when((local >= 0) & (local < near))
-        def _():
-            rank = count_ref[local]
-            slot_ref[local * slots + rank] = row_ref[b] * (halves * ncb) + col_ref[b]
-            count_ref[local] = rank + 1
-
+        mine = (local >= 0) & (local < near)
+        local = jnp.where(mine, local, near)
+        rank = count_ref[local]
+        slot_ref[local * slots + rank] = row_ref[b] * (halves * ncb) + col_ref[b]
+        count_ref[local] = rank + mine.astype(jnp.int32)
         return carry
 
     lax.fori_loop(0, owner_ref.shape[0], put, 0, unroll=8)
@@ -72,13 +70,13 @@
 
 
 def owner_kernel(
-    tiles_ref, left_stats_ref, right_stats_ref, left_root_ref, right_root_ref, *refs, mine
+    tiles_ref, left_stats_ref, right_stats_ref, right_root_ref, left_root_ref, *refs, mine
 ):
     if mine:
-        direction_hbm, left_hbm, right_hbm, staged_ref, stats_ref, stats_sem = refs[:6]
+        direction_hbm, left_hbm, right_hbm, staged_ref, roots_ref, roots_sem = refs[:6]
     else:
         direction_hbm, left_hbm, right_hbm = refs[3:6]
-        stats_ref = right_stats_ref
+        roots_ref = left_root_ref
     block_ref, columns_ref, direction_ref, left_ref, right_ref, out_sem = refs[-6:]
     near, groups, halves = tiles_ref.shape[:3]
     order = block_ref.shape[0]
@@ -90,8 +88,8 @@
     copies = []
     if mine:
         copies = [
-            pltpu.make_async_copy(right_stats_ref.at[k], stats_ref, stats_sem.at[0]),
-            pltpu.make_async_copy(right_stats_ref.at[1 - k], staged_ref, stats_sem.at[1]),
+            pltpu.make_async_copy(left_root_ref.at[k, my_rows, :], roots_ref, roots_sem.at[0]),
+            pltpu.make_async_copy(left_root_ref.at[1 - k, my_rows, :], staged_ref, roots_sem.at[1]),
         ]
         for copy in copies:
             copy.start()
@@ -117,16 +115,16 @@
         two_bands, block, (((0,), (0,)), ((), ())), preferred_element_type=jnp.float32
     )
     right = columns_ref[pl.ds(pl.multiple_of(me * band - start, band), band), :]
-    for copy in copies[:1]:
-        copy.wait()
-    right_ref[...] = 0.8 * stats_ref[...] + (0.2 / order) * right
+    right_ref[...] = 0.8 * right_stats_ref[k] + (0.2 / order) * right
     results[1].start()
     mixed = jnp.dot(block, right_root_ref[k], preferred_element_type=jnp.float32).astype(jnp.bfloat16)
+    for copy in copies:
+        copy.wait()
     direction_ref[...] = jnp.dot(
-        left_root_ref[k, my_rows, :], mixed, preferred_element_type=jnp.float32
+        roots_ref[...], mixed, preferred_element_type=jnp.float32
     ).astype(jnp.bfloat16)
     results[2].start()
-    for copy in copies[1:] + results:
+    for copy in results:
         copy.wait()
 
 
@@ -137,10 +135,10 @@
     out_specs = (hbm,) * 3
     scratch = []
     if mine:
-        in_specs = vmem(2) + [hbm] + vmem(2)
-        out_shape += (pltpu.VMEM((band, order), f32),)
+        in_specs = vmem(4) + [hbm]
+        out_shape += (pltpu.VMEM((band, order), bf16),)
         out_specs += tuple(vmem(1))
-        scratch = [pltpu.VMEM((band, order), f32), pltpu.SemaphoreType.DMA((2,))]
+        scratch = [pltpu.VMEM((band, order), bf16), pltpu.SemaphoreType.DMA((2,))]
         aliases = {}
     else:
         in_specs = vmem(5) + [hbm] * 3
@@ -173,12 +171,10 @@
 ):
     slots, order, _ = left_root.shape
     band = left_stats.shape[1]
-    local_rows, cols = replica_grads.shape[1:]
-    ncb = cols // order
+    ncb = replica_grads.shape[2] // order
     groups, halves = lax.axis_size("x"), lax.axis_size("core")
     replicas = groups * halves
     near = lax.axis_size("zl") * lax.axis_size("y")
-    cubes = lax.axis_size("cube")
     bf16 = jnp.bfloat16
     smem = pl.BlockSpec(memory_space=pltpu.SMEM)
 
@@ -186,14 +182,14 @@
         functools.partial(cut_kernel, near=near, slots=slots, ncb=ncb),
         out_shape=(
             pltpu.VMEM((replicas, ncb, TILE_ROWS, LANES), bf16),
-            jax.ShapeDtypeStruct((near * slots,), jnp.int32),
+            jax.ShapeDtypeStruct(((near + 1) * slots,), jnp.int32),
         ),
         in_specs=[pl.BlockSpec(memory_space=pl.ANY)] * 4,
         out_specs=(vmem(1)[0], smem),
         scratch_shapes=[pltpu.SMEM(block_owner.shape, jnp.int32)] * 3
         + [
             pltpu.VMEM(replica_grads.shape, bf16),
-            pltpu.SMEM((near,), jnp.int32),
+            pltpu.SMEM((near + 1,), jnp.int32),
             pltpu.SemaphoreType.DMA((3,)),
             pltpu.SemaphoreType.DMA,
         ],
@@ -218,14 +214,12 @@
     own = own.reshape(near, groups, halves, TILE_ROWS, LANES)
     other = lax.ppermute(own, "core", [(0, 1), (1, 0)])
 
-    left_stats, left_root, right_root = (
-        pltpu.with_memory_space_constraint(a, pltpu.VMEM) for a in (left_stats, left_root, right_root)
-    )
-    right_stats = pltpu.with_memory_space_constraint(right_stats, pltpu.HBM)
-    operands = own, left_stats, right_stats, left_root, right_root
-    *results, staged = owner_call(True, operands, slots, band, order)
-    operands = other, left_stats, staged, left_root, right_root
-    return owner_call(False, (*operands, *results), slots, band, order)
+    operands = tuple(
+        pltpu.with_memory_space_constraint(a, pltpu.VMEM) for a in (left_stats, right_stats, right_root)
+    )
+    left_root = pltpu.with_memory_space_constraint(left_root, pltpu.HBM)
+    *results, staged = owner_call(True, (own, *operands, left_root), slots, band, order)
+    return owner_call(False, (other, *operands, staged, *results), slots, band, order)
 
 
 def solution(mesh):

time: 97.6 us -> 97.3 us (level)
  no operation moved by 1% of the time
where the time goes in v8:
time: 97.3 us; the launch traced here: 97 us
  blocking collectives  86 us (88%)
  Pallas kernels  6.44 us (7%)
  starting transfers between devices  3.74 us (4%)
    all_gather x1, blocking collectives, per_device(): shares = lax.all_gather(summed, ('cube', 'core'), axis=0, tiled=True)  33.9 us
    all_to_all x1, blocking collectives, per_device(): own = lax.all_to_all(picked, ('zl', 'y', 'x'), 0, 0, tiled=True)  27.5 us
    all_to_all x1, blocking collectives, per_device(): received = lax.all_to_all(parts, ('x', 'core'), 0, 0, tiled=True)  24.6 us
    ppermute x1, starting transfers between devices, per_device(): other = lax.ppermute(own, 'core', [(0, 1), (1, 0)])  3.74 us
    pallas_call x2, Pallas kernels, owner_call(): pl.pallas_call(functools.partial(owner_kernel, mine=mine), out_shape=out_...  3.63 us
  transfers between devices with their start and end apart: 1, of which 0 were waited for; matrix products, arithmetic and copies ran while one was open for 0% of the time, Pallas kernels for 2%

profile of v8, /device:TPU:1, one launch (start us, length us, event | category | flops | bytes accessed | tf_op | source)
XLA Modules:
  0.0 97.0 jit_solution(5850921416771641028)
XLA Ops:
  0.6 1.9 %cut.1 = (bf16[8,12,16,128]{3,2,1,0:T(8,128)(2,1)S(1)}, s32[34]{0:T(128)}) custom-call(s32[96]{0:T(128)} %owner_hbm.1, s32[96]{0:T(128)} %row_hbm.1, s32[96]{0:T(128)} %col_hbm.1, bf16[1,32,6144]{2,1,0:T(8,128)(2,1)} %grads_hbm.1), custom_call_target="tpu_custom_call" | custom-call | tf_op jit(solution)/shard_map/cut/pallas_call | solution.py:181
  2.6 24.6 %all_to_all.10 = bf16[8,12,16,128]{3,2,1,0:T(8,128)(2,1)S(1)} all-to-all(bf16[8,12,16,128]{3,2,1,0:T(8,128)(2,1)S(1)} %get-tuple-element.10), channel_id=1, replica_groups=mesh['cube'=8,'zl'=4,'y'=4,'x'=4,'core'=2] {'x','core'}, dimensions={0} | all-to-all | bytes 786432 | tf_op jit(solution)/shard_map/all_to_all | solution.py:199
  27.2 0.1 reduce_sum.12
  27.3 33.9 %all_gather.3.shares_ref = bf16[192,16,128]{2,1,0:T(8,128)(2,1)S(1)} all-gather(bf16[12,16,128]{2,1,0:T(8,128)(2,1)S(1)} %reduce_sum.12), channel_id=1, replica_groups=mesh['cube'=8,'zl'=4,'y'=4,'x'=4,'core'=2] {'cube','core'}, dimensions={0}, use_global_device_ids=true | all-gather | bytes 835584 | tf_op jit(solution)/shard_map/all_gather | solution.py:201
  61.2 0.0 copy-start
  61.2 0.9 pick.1
  62.1 0.0 copy-start.1
  62.1 0.0 copy-start.2
  62.1 27.5 %all_to_all.11 = bf16[64,2,16,128]{3,2,1,0:T(8,128)(2,1)S(1)} all-to-all(bf16[64,2,16,128]{3,2,1,0:T(8,128)(2,1)S(1)} %bitcast.2), channel_id=1, replica_groups=mesh['cube'=8,'zl'=4,'y'=4,'x'=4,'core'=2] {'zl','y','x'}, dimensions={0} | all-to-all | bytes 1048576 | tf_op jit(solution)/shard_map/all_to_all | solution.py:213
  89.6 3.7 %collective-permute-start = (bf16[16,4,2,16,128]{4,3,2,1,0:T(8,128)(2,1)S(1)}, bf16[16,4,2,16,128]{4,3,2,1,0:T(8,128)(2,1)S(1)}, u32[]{:S(2)}, u32[]{:S(2)}) collective-permute-start(bf16[16,4,2,16,128]{4,3,2,1,0:T(8,128)(2,1)S(1)} %bitcast.3), channel_id=1, source_target_pairs={{0,1},{1,0},{2,3},{3,2},{4,5},{5,4},{6,7},{7,6},{8,9},{9,8},{10,11... | collective-permute-start | bytes 1572872 | tf_op jit(solution)/shard_map/ppermute | solution.py:215
  93.3 0.0 copy-done
  93.3 0.0 copy-done.1
  93.3 0.0 copy-done.2
  93.4 2.1 %own.1 = (bf16[2,64,512]{2,1,0:T(8,128)(2,1)}, f32[2,64,512]{2,1,0:T(8,128)}, f32[2,64,512]{2,1,0:T(8,128)}, bf16[64,512]{1,0:T(8,128)(2,1)S(1)}) custom-call(bf16[16,4,2,16,128]{4,3,2,1,0:T(8,128)(2,1)S(1)} %bitcast.4, f32[2,64,512]{2,1,0:T(8,128)S(1)} %copy-done.1, f32[2,64,512]{2,1,0:T(8,128)S(1)} %copy-done.2, bf16[2,512,512]{2,1,0:T(8,128)(2,1)S(1)} %copy-done, ...), custom_call_target="tpu_custom_call" | custom-call | flops 402653184 | bytes 2097152 | tf_op jit(solution)/shard_map/own/pallas_call | solution.py:154
  95.5 0.0 collective-permute-done.tiles_ref
  95.5 1.5 %other.1 = (bf16[2,64,512]{2,1,0:T(8,128)(2,1)}, f32[2,64,512]{2,1,0:T(8,128)}, f32[2,64,512]{2,1,0:T(8,128)}) custom-call(bf16[16,4,2,16,128]{4,3,2,1,0:T(8,128)(2,1)S(1)} %collective-permute-done.tiles_ref, f32[2,64,512]{2,1,0:T(8,128)S(1)} %copy-done.1, f32[2,64,512]{2,1,0:T(8,128)S(1)} %copy-done.2, ...), custom_call_target="tpu_custom_call", output_to_operand_aliasing={{0}: (5, {}), {1}: (6, {}), {2}: (7, {})} | custom-call | flops 402653184 | bytes 2097152 | tf_op jit(solution)/shard_map/other/pallas_call | solution.py:154
Async XLA Ops:
  61.2 32.1 %copy-start = (bf16[2,512,512]{2,1,0:T(8,128)(2,1)S(1)}, bf16[2,512,512]{2,1,0:T(8,128)(2,1)}, u32[]{:S(2)}) copy-start(bf16[2,512,512]{2,1,0:T(8,128)(2,1)} %right_root_ref.3) | copy-start | bytes 3145732
  62.1 31.3 %copy-start.1 = (f32[2,64,512]{2,1,0:T(8,128)S(1)}, f32[2,64,512]{2,1,0:T(8,128)}, u32[]{:S(2)}) copy-start(f32[2,64,512]{2,1,0:T(8,128)} %left_stats_ref.3) | copy-start | bytes 786436
  62.1 31.2 %copy-start.2 = (f32[2,64,512]{2,1,0:T(8,128)S(1)}, f32[2,64,512]{2,1,0:T(8,128)}, u32[]{:S(2)}) copy-start(f32[2,64,512]{2,1,0:T(8,128)} %right_stats_ref.3) | copy-start | bytes 786436
  89.6 5.9 %collective-permute-start = (bf16[16,4,2,16,128]{4,3,2,1,0:T(8,128)(2,1)S(1)}, bf16[16,4,2,16,128]{4,3,2,1,0:T(8,128)(2,1)S(1)}, u32[]{:S(2)}, u32[]{:S(2)}) collective-permute-start(bf16[16,4,2,16,128]{4,3,2,1,0:T(8,128)(2,1)S(1)} %bitcast.3), channel_id=1, source_target_pairs={{0,1},{1,0},{2,3},{3,2},{4,5},{5,4},{6,7},{7,6},{8,9},{9,8},{10,11... | collective-permute-start | bytes 1572872 | tf_op jit(solution)/shard_map/ppermute | solution.py:215

commit v9 on v8

--- a/solution.py
+++ b/solution.py
@@ -19,14 +19,14 @@
     owner_hbm, row_hbm, col_hbm, grads_hbm, parts_ref, slot_ref,
     owner_ref, row_ref, col_ref, grads_ref, count_ref, table_sem, grads_sem, *, near, slots, ncb,
 ):
-    grads_copy = pltpu.make_async_copy(grads_hbm, grads_ref, grads_sem)
-    grads_copy.start()
     table_copies = [
         pltpu.make_async_copy(source, target, table_sem.at[i])
         for i, (source, target) in enumerate(((owner_hbm, owner_ref), (row_hbm, row_ref), (col_hbm, col_ref)))
     ]
     for copy in table_copies:
         copy.start()
+    grads_copy = pltpu.make_async_copy(grads_hbm, grads_ref, grads_sem)
+    grads_copy.start()
     halves = grads_ref.shape[1] // TILE_ROWS
     for i in range(slot_ref.shape[0]):
         slot_ref[i] = -1
@@ -117,14 +117,14 @@
     right = columns_ref[pl.ds(pl.multiple_of(me * band - start, band), band), :]
     right_ref[...] = 0.8 * right_stats_ref[k] + (0.2 / order) * right
     results[1].start()
-    mixed = jnp.dot(block, right_root_ref[k], preferred_element_type=jnp.float32).astype(jnp.bfloat16)
-    for copy in copies:
+    for copy in copies[:1]:
         copy.wait()
+    mixed = jnp.dot(roots_ref[...], block, preferred_element_type=jnp.float32).astype(jnp.bfloat16)
     direction_ref[...] = jnp.dot(
-        roots_ref[...], mixed, preferred_element_type=jnp.float32
+        mixed, right_root_ref[k], preferred_element_type=jnp.float32
     ).astype(jnp.bfloat16)
     results[2].start()
-    for copy in results:
+    for copy in copies[1:] + results:
         copy.wait()
 
 
@@ -160,7 +160,7 @@
         input_output_aliases=aliases,
         compiler_params=pltpu.CompilerParams(vmem_limit_bytes=32 * 1024 * 1024),
         cost_estimate=pl.CostEstimate(
-            flops=2 * order * order * (order + 4 * band), bytes_accessed=8 * order * order, transcendentals=0
+            flops=2 * order * order * 5 * band, bytes_accessed=8 * order * order, transcendentals=0
         ),
         name="own" if mine else "other",
     )(*operands)

time: 97.3 us -> 96.9 us (level)
  no operation moved by 1% of the time
where the time goes in v9:
time: 96.9 us; the launch traced here: 96.6 us
  blocking collectives  86 us (89%)
  Pallas kernels  6.02 us (6%)
  starting transfers between devices  3.74 us (4%)
    all_gather x1, blocking collectives, per_device(): shares = lax.all_gather(summed, ('cube', 'core'), axis=0, tiled=True)  33.9 us
    all_to_all x1, blocking collectives, per_device(): own = lax.all_to_all(picked, ('zl', 'y', 'x'), 0, 0, tiled=True)  27.5 us
    all_to_all x1, blocking collectives, per_device(): received = lax.all_to_all(parts, ('x', 'core'), 0, 0, tiled=True)  24.6 us
    ppermute x1, starting transfers between devices, per_device(): other = lax.ppermute(own, 'core', [(0, 1), (1, 0)])  3.74 us
    pallas_call x2, Pallas kernels, owner_call(): pl.pallas_call(functools.partial(owner_kernel, mine=mine), out_shape=out_...  3.34 us
  transfers between devices with their start and end apart: 1, of which 0 were waited for; matrix products, arithmetic and copies ran while one was open for 0% of the time, Pallas kernels for 2%

profile of v9, /device:TPU:1, one launch (start us, length us, event | category | flops | bytes accessed | tf_op | source)
XLA Modules:
  0.0 96.6 jit_solution(15654535219256059453)
XLA Ops:
  0.6 1.8 %cut.1 = (bf16[8,12,16,128]{3,2,1,0:T(8,128)(2,1)S(1)}, s32[34]{0:T(128)}) custom-call(s32[96]{0:T(128)} %owner_hbm.1, s32[96]{0:T(128)} %row_hbm.1, s32[96]{0:T(128)} %col_hbm.1, bf16[1,32,6144]{2,1,0:T(8,128)(2,1)} %grads_hbm.1), custom_call_target="tpu_custom_call" | custom-call | tf_op jit(solution)/shard_map/cut/pallas_call | solution.py:181
  2.4 24.6 %all_to_all.10 = bf16[8,12,16,128]{3,2,1,0:T(8,128)(2,1)S(1)} all-to-all(bf16[8,12,16,128]{3,2,1,0:T(8,128)(2,1)S(1)} %get-tuple-element.10), channel_id=1, replica_groups=mesh['cube'=8,'zl'=4,'y'=4,'x'=4,'core'=2] {'x','core'}, dimensions={0} | all-to-all | bytes 786432 | tf_op jit(solution)/shard_map/all_to_all | solution.py:199
  27.1 0.1 reduce_sum.12
  27.1 33.9 %all_gather.3.shares_ref = bf16[192,16,128]{2,1,0:T(8,128)(2,1)S(1)} all-gather(bf16[12,16,128]{2,1,0:T(8,128)(2,1)S(1)} %reduce_sum.12), channel_id=1, replica_groups=mesh['cube'=8,'zl'=4,'y'=4,'x'=4,'core'=2] {'cube','core'}, dimensions={0}, use_global_device_ids=true | all-gather | bytes 835584 | tf_op jit(solution)/shard_map/all_gather | solution.py:201
  61.1 0.0 copy-start
  61.1 0.9 pick.1
  62.0 0.0 copy-start.1
  62.0 0.0 copy-start.2
  62.0 27.5 %all_to_all.11 = bf16[64,2,16,128]{3,2,1,0:T(8,128)(2,1)S(1)} all-to-all(bf16[64,2,16,128]{3,2,1,0:T(8,128)(2,1)S(1)} %bitcast.2), channel_id=1, replica_groups=mesh['cube'=8,'zl'=4,'y'=4,'x'=4,'core'=2] {'zl','y','x'}, dimensions={0} | all-to-all | bytes 1048576 | tf_op jit(solution)/shard_map/all_to_all | solution.py:213
  89.4 3.7 %collective-permute-start = (bf16[16,4,2,16,128]{4,3,2,1,0:T(8,128)(2,1)S(1)}, bf16[16,4,2,16,128]{4,3,2,1,0:T(8,128)(2,1)S(1)}, u32[]{:S(2)}, u32[]{:S(2)}) collective-permute-start(bf16[16,4,2,16,128]{4,3,2,1,0:T(8,128)(2,1)S(1)} %bitcast.3), channel_id=1, source_target_pairs={{0,1},{1,0},{2,3},{3,2},{4,5},{5,4},{6,7},{7,6},{8,9},{9,8},{10,11... | collective-permute-start | bytes 1572872 | tf_op jit(solution)/shard_map/ppermute | solution.py:215
  93.2 0.0 copy-done
  93.2 0.0 copy-done.1
  93.2 0.0 copy-done.2
  93.2 2.0 %own.1 = (bf16[2,64,512]{2,1,0:T(8,128)(2,1)}, f32[2,64,512]{2,1,0:T(8,128)}, f32[2,64,512]{2,1,0:T(8,128)}, bf16[64,512]{1,0:T(8,128)(2,1)S(1)}) custom-call(bf16[16,4,2,16,128]{4,3,2,1,0:T(8,128)(2,1)S(1)} %bitcast.4, f32[2,64,512]{2,1,0:T(8,128)S(1)} %copy-done.1, f32[2,64,512]{2,1,0:T(8,128)S(1)} %copy-done.2, bf16[2,512,512]{2,1,0:T(8,128)(2,1)S(1)} %copy-done, ...), custom_call_target="tpu_custom_call" | custom-call | flops 167772160 | bytes 2097152 | tf_op jit(solution)/shard_map/own/pallas_call | solution.py:154
  95.3 0.0 collective-permute-done.tiles_ref
  95.3 1.3 %other.1 = (bf16[2,64,512]{2,1,0:T(8,128)(2,1)}, f32[2,64,512]{2,1,0:T(8,128)}, f32[2,64,512]{2,1,0:T(8,128)}) custom-call(bf16[16,4,2,16,128]{4,3,2,1,0:T(8,128)(2,1)S(1)} %collective-permute-done.tiles_ref, f32[2,64,512]{2,1,0:T(8,128)S(1)} %copy-done.1, f32[2,64,512]{2,1,0:T(8,128)S(1)} %copy-done.2, ...), custom_call_target="tpu_custom_call", output_to_operand_aliasing={{0}: (5, {}), {1}: (6, {}), {2}: (7, {})} | custom-call | flops 167772160 | bytes 2097152 | tf_op jit(solution)/shard_map/other/pallas_call | solution.py:154
Async XLA Ops:
  61.1 32.1 %copy-start = (bf16[2,512,512]{2,1,0:T(8,128)(2,1)S(1)}, bf16[2,512,512]{2,1,0:T(8,128)(2,1)}, u32[]{:S(2)}) copy-start(bf16[2,512,512]{2,1,0:T(8,128)(2,1)} %right_root_ref.3) | copy-start | bytes 3145732
  62.0 31.3 %copy-start.1 = (f32[2,64,512]{2,1,0:T(8,128)S(1)}, f32[2,64,512]{2,1,0:T(8,128)}, u32[]{:S(2)}) copy-start(f32[2,64,512]{2,1,0:T(8,128)} %left_stats_ref.3) | copy-start | bytes 786436
  62.0 31.2 %copy-start.2 = (f32[2,64,512]{2,1,0:T(8,128)S(1)}, f32[2,64,512]{2,1,0:T(8,128)}, u32[]{:S(2)}) copy-start(f32[2,64,512]{2,1,0:T(8,128)} %right_stats_ref.3) | copy-start | bytes 786436
  89.4 5.8 %collective-permute-start = (bf16[16,4,2,16,128]{4,3,2,1,0:T(8,128)(2,1)S(1)}, bf16[16,4,2,16,128]{4,3,2,1,0:T(8,128)(2,1)S(1)}, u32[]{:S(2)}, u32[]{:S(2)}) collective-permute-start(bf16[16,4,2,16,128]{4,3,2,1,0:T(8,128)(2,1)S(1)} %bitcast.3), channel_id=1, source_target_pairs={{0,1},{1,0},{2,3},{3,2},{4,5},{5,4},{6,7},{7,6},{8,9},{9,8},{10,11... | collective-permute-start | bytes 1572872 | tf_op jit(solution)/shard_map/ppermute | solution.py:215

commit v10 on v7

--- a/solution.py
+++ b/solution.py
@@ -19,14 +19,14 @@
     owner_hbm, row_hbm, col_hbm, grads_hbm, parts_ref, slot_ref,
     owner_ref, row_ref, col_ref, grads_ref, count_ref, table_sem, grads_sem, *, near, slots, ncb,
 ):
-    grads_copy = pltpu.make_async_copy(grads_hbm, grads_ref, grads_sem)
-    grads_copy.start()
     table_copies = [
         pltpu.make_async_copy(source, target, table_sem.at[i])
         for i, (source, target) in enumerate(((owner_hbm, owner_ref), (row_hbm, row_ref), (col_hbm, col_ref)))
     ]
     for copy in table_copies:
         copy.start()
+    grads_copy = pltpu.make_async_copy(grads_hbm, grads_ref, grads_sem)
+    grads_copy.start()
     halves = grads_ref.shape[1] // TILE_ROWS
     for i in range(slot_ref.shape[0]):
         slot_ref[i] = -1
@@ -57,9 +57,7 @@
                 ]
 
 
-def pick_kernel(slot_ref, shares_ref, stats_hbm, picked_ref, stats_ref, stats_sem, *, ncb):
-    stats_copy = pltpu.make_async_copy(stats_hbm, stats_ref, stats_sem)
-    stats_copy.start()
+def pick_kernel(slot_ref, shares_ref, _, picked_ref, *, ncb):
     near, groups, halves = picked_ref.shape[:3]
     core = lax.axis_index("core")
     for o in range(near):
@@ -69,7 +67,6 @@
             tile = jnp.where(at >= 0, tile, jnp.zeros_like(tile))
             for x in range(groups):
                 picked_ref[o, x, half] = tile
-    stats_copy.wait()
 
 
 def owner_kernel(
@@ -108,9 +105,9 @@
     right = columns_ref[pl.ds(pl.multiple_of(me * band - start, band), band), :]
     right_ref[...] = 0.8 * right_stats_ref[k] + (0.2 / order) * right
     results[1].start()
-    mixed = jnp.dot(block, right_root_ref[k], preferred_element_type=jnp.float32).astype(jnp.bfloat16)
+    mixed = jnp.dot(left_root_ref[k, my_rows, :], block, preferred_element_type=jnp.float32).astype(jnp.bfloat16)
     direction_ref[...] = jnp.dot(
-        left_root_ref[k, my_rows, :], mixed, preferred_element_type=jnp.float32
+        mixed, right_root_ref[k], preferred_element_type=jnp.float32
     ).astype(jnp.bfloat16)
     results[2].start()
     for copy in results:
@@ -138,7 +135,7 @@
         input_output_aliases=aliases,
         compiler_params=pltpu.CompilerParams(vmem_limit_bytes=32 * 1024 * 1024),
         cost_estimate=pl.CostEstimate(
-            flops=2 * order * order * (order + 4 * band), bytes_accessed=8 * order * order, transcendentals=0
+            flops=2 * order * order * 5 * band, bytes_accessed=8 * order * order, transcendentals=0
         ),
         name="own" if mine else "other",
     )(*operands)
@@ -179,27 +176,24 @@
     shares = lax.all_gather(summed, ("cube", "core"), axis=0, tiled=True)
     shares = pltpu.with_memory_space_constraint(shares, pltpu.VMEM)
 
-    picked, right_stats = pl.pallas_call(
+    left_stats, right_stats, left_root, right_root = (
+        pltpu.with_memory_space_constraint(a, pltpu.VMEM)
+        for a in (left_stats, right_stats, left_root, right_root)
+    )
+    picked = pl.pallas_call(
         functools.partial(pick_kernel, ncb=ncb),
-        out_shape=(
-            pltpu.VMEM((near, groups, halves, TILE_ROWS, LANES), bf16),
-            pltpu.VMEM(right_stats.shape, jnp.float32),
-        ),
-        in_specs=[smem] + vmem(1) + [pl.BlockSpec(memory_space=pl.ANY)],
-        out_specs=tuple(vmem(2)),
-        scratch_shapes=[pltpu.SemaphoreType.DMA],
+        out_shape=pltpu.VMEM((near, groups, halves, TILE_ROWS, LANES), bf16),
+        in_specs=[smem] + vmem(2),
+        out_specs=vmem(1)[0],
         name="pick",
-    )(slot, shares, right_stats)
+    )(slot, shares, right_root)
 
     picked = picked.reshape(near * groups, halves, TILE_ROWS, LANES)
     own = lax.all_to_all(picked, ("zl", "y", "x"), 0, 0, tiled=True)
     own = own.reshape(near, groups, halves, TILE_ROWS, LANES)
     other = lax.ppermute(own, "core", [(0, 1), (1, 0)])
 
-    operands = tuple(
-        pltpu.with_memory_space_constraint(a, pltpu.VMEM)
-        for a in (left_stats, right_stats, left_root, right_root)
-    )
+    operands = left_stats, right_stats, left_root, right_root
     results = owner_call(True, (own, *operands), slots, band, order)
     return owner_call(False, (other, *operands, *results), slots, band, order)
 

time: 97.7 us -> 96.4 us (0.987)
  Pallas kernels: 6.72 us -> 5.3 us
  transfers between devices with their start and end apart: 1 -> 1, of which waited for: 0 -> 1; matrix products, arithmetic and copies ran while one was open for 0% -> 0% of each run, Pallas kernels for 2% -> 1%
where the time goes in v10:
time: 96.4 us; the launch traced here: 96.2 us
  blocking collectives  86.2 us (89%)
  Pallas kernels  5.3 us (5%)
  starting transfers between devices  3.74 us (4%)
    all_gather x1, blocking collectives, per_device(): shares = lax.all_gather(summed, ('cube', 'core'), axis=0, tiled=True)  33.9 us
    all_to_all x1, blocking collectives, per_device(): own = lax.all_to_all(picked, ('zl', 'y', 'x'), 0, 0, tiled=True)  27.5 us
    all_to_all x1, blocking collectives, per_device(): received = lax.all_to_all(parts, ('x', 'core'), 0, 0, tiled=True)  24.8 us
    ppermute x1, starting transfers between devices, per_device(): other = lax.ppermute(own, 'core', [(0, 1), (1, 0)])  3.74 us
    pallas_call x2, Pallas kernels, owner_call(): pl.pallas_call(functools.partial(owner_kernel, mine=mine), out_shape=tupl...  2.62 us
  transfers between devices with their start and end apart: 1, of which 1 were waited for; matrix products, arithmetic and copies ran while one was open for 0% of the time, Pallas kernels for 1%

profile of v10, /device:TPU:1, one launch (start us, length us, event | category | flops | bytes accessed | tf_op | source)
XLA Modules:
  0.0 96.2 jit_solution(17394149869485397814)
XLA Ops:
  0.6 1.8 %cut.1 = (bf16[8,12,16,128]{3,2,1,0:T(8,128)(2,1)S(1)}, s32[34]{0:T(128)}) custom-call(s32[96]{0:T(128)} %owner_hbm.1, s32[96]{0:T(128)} %row_hbm.1, s32[96]{0:T(128)} %col_hbm.1, bf16[1,32,6144]{2,1,0:T(8,128)(2,1)} %grads_hbm.1), custom_call_target="tpu_custom_call" | custom-call | tf_op jit(solution)/shard_map/cut/pallas_call | solution.py:156
  2.4 0.0 copy-start
  2.5 24.8 %all_to_all.10 = bf16[8,12,16,128]{3,2,1,0:T(8,128)(2,1)S(1)} all-to-all(bf16[8,12,16,128]{3,2,1,0:T(8,128)(2,1)S(1)} %get-tuple-element.9), channel_id=1, replica_groups=mesh['cube'=8,'zl'=4,'y'=4,'x'=4,'core'=2] {'x','core'}, dimensions={0} | all-to-all | bytes 786432 | tf_op jit(solution)/shard_map/all_to_all | solution.py:174
  27.2 0.1 reduce_sum.12
  27.3 33.9 %all_gather.3.shares_ref = bf16[192,16,128]{2,1,0:T(8,128)(2,1)S(1)} all-gather(bf16[12,16,128]{2,1,0:T(8,128)(2,1)S(1)} %reduce_sum.12), channel_id=1, replica_groups=mesh['cube'=8,'zl'=4,'y'=4,'x'=4,'core'=2] {'cube','core'}, dimensions={0}, use_global_device_ids=true | all-gather | bytes 835584 | tf_op jit(solution)/shard_map/all_gather | solution.py:176
  61.2 0.0 copy-done
  61.2 0.0 copy-start.2
  61.2 0.0 copy-start.3
  61.2 0.9 pick.1
  62.1 0.0 copy-start.1
  62.1 27.5 %all_to_all.11 = bf16[64,2,16,128]{3,2,1,0:T(8,128)(2,1)S(1)} all-to-all(bf16[64,2,16,128]{3,2,1,0:T(8,128)(2,1)S(1)} %bitcast.2), channel_id=1, replica_groups=mesh['cube'=8,'zl'=4,'y'=4,'x'=4,'core'=2] {'zl','y','x'}, dimensions={0} | all-to-all | bytes 1048576 | tf_op jit(solution)/shard_map/all_to_all | solution.py:192
  89.6 3.7 %collective-permute-start = (bf16[16,4,2,16,128]{4,3,2,1,0:T(8,128)(2,1)S(1)}, bf16[16,4,2,16,128]{4,3,2,1,0:T(8,128)(2,1)S(1)}, u32[]{:S(2)}, u32[]{:S(2)}) collective-permute-start(bf16[16,4,2,16,128]{4,3,2,1,0:T(8,128)(2,1)S(1)} %bitcast.3), channel_id=1, source_target_pairs={{0,1},{1,0},{2,3},{3,2},{4,5},{5,4},{6,7},{7,6},{8,9},{9,8},{10,11... | collective-permute-start | bytes 1572872 | tf_op jit(solution)/shard_map/ppermute | solution.py:194
  93.3 0.0 copy-done.2
  93.3 0.0 copy-done.3
  93.3 0.0 copy-done.1
  93.4 1.3 %own.1 = (bf16[2,64,512]{2,1,0:T(8,128)(2,1)}, f32[2,64,512]{2,1,0:T(8,128)}, f32[2,64,512]{2,1,0:T(8,128)}) custom-call(bf16[16,4,2,16,128]{4,3,2,1,0:T(8,128)(2,1)S(1)} %bitcast.4, f32[2,64,512]{2,1,0:T(8,128)S(1)} %copy-done.2, f32[2,64,512]{2,1,0:T(8,128)S(1)} %copy-done.3, bf16[2,512,512]{2,1,0:T(8,128)(2,1)S(1)} %copy-done.1, ...), custom_call_target="tpu_custom_call" | custom-call | flops 167772160 | bytes 2097152 | tf_op jit(solution)/shard_map/own/pallas_call | solution.py:129
  94.7 0.2 collective-permute-done.tiles_ref
  94.8 1.3 %other.1 = (bf16[2,64,512]{2,1,0:T(8,128)(2,1)}, f32[2,64,512]{2,1,0:T(8,128)}, f32[2,64,512]{2,1,0:T(8,128)}) custom-call(bf16[16,4,2,16,128]{4,3,2,1,0:T(8,128)(2,1)S(1)} %collective-permute-done.tiles_ref, f32[2,64,512]{2,1,0:T(8,128)S(1)} %copy-done.2, f32[2,64,512]{2,1,0:T(8,128)S(1)} %copy-done.3, ...), custom_call_target="tpu_custom_call", output_to_operand_aliasing={{0}: (5, {}), {1}: (6, {}), {2}: (7, {})} | custom-call | flops 167772160 | bytes 2097152 | tf_op jit(solution)/shard_map/other/pallas_call | solution.py:129
Async XLA Ops:
  2.4 58.8 %copy-start = (bf16[2,512,512]{2,1,0:T(8,128)(2,1)S(1)}, bf16[2,512,512]{2,1,0:T(8,128)(2,1)}, u32[]{:S(2)}) copy-start(bf16[2,512,512]{2,1,0:T(8,128)(2,1)} %right_root_ref.3) | copy-start | bytes 3145732
  61.2 32.1 %copy-start.2 = (f32[2,64,512]{2,1,0:T(8,128)S(1)}, f32[2,64,512]{2,1,0:T(8,128)}, u32[]{:S(2)}) copy-start(f32[2,64,512]{2,1,0:T(8,128)} %left_stats_ref.3) | copy-start | bytes 786436
  61.2 32.1 %copy-start.3 = (f32[2,64,512]{2,1,0:T(8,128)S(1)}, f32[2,64,512]{2,1,0:T(8,128)}, u32[]{:S(2)}) copy-start(f32[2,64,512]{2,1,0:T(8,128)} %right_stats_ref.3) | copy-start | bytes 786436
  62.1 31.2 %copy-start.1 = (bf16[2,512,512]{2,1,0:T(8,128)(2,1)S(1)}, bf16[2,512,512]{2,1,0:T(8,128)(2,1)}, u32[]{:S(2)}) copy-start(bf16[2,512,512]{2,1,0:T(8,128)(2,1)} %left_root_ref.3) | copy-start | bytes 3145732
  89.6 5.3 %collective-permute-start = (bf16[16,4,2,16,128]{4,3,2,1,0:T(8,128)(2,1)S(1)}, bf16[16,4,2,16,128]{4,3,2,1,0:T(8,128)(2,1)S(1)}, u32[]{:S(2)}, u32[]{:S(2)}) collective-permute-start(bf16[16,4,2,16,128]{4,3,2,1,0:T(8,128)(2,1)S(1)} %bitcast.3), channel_id=1, source_target_pairs={{0,1},{1,0},{2,3},{3,2},{4,5},{5,4},{6,7},{7,6},{8,9},{9,8},{10,11... | collective-permute-start | bytes 1572872 | tf_op jit(solution)/shard_map/ppermute | solution.py:194
